TPU v7x, 128 devices: a whole 4x4x4 slice. The times are simulated.
128 devices in a mesh: view: 4 (over x), pix: 32 (over y, z, core).
Axes of the slice: x: 4, y: 4, z: 4, core: 2. Of those that a mesh axis runs over, the one named last changes fastest.
Arguments:
- centers: float32 [3, 1048576], P(None, ('view', 'pix'))
- log_scales: float32 [3, 1048576], P(None, ('view', 'pix')), may hold values from -4.8 to -3.5
- rotations: float32 [4, 1048576], P(None, ('view', 'pix')), may hold values from 0.3 to 1.5
- logits: float32 [1048576], P(('view', 'pix')), may hold values from -7 to -4
- harmonic_coeffs: float32 [48, 1048576], P(None, ('view', 'pix')), may hold values from -3 to 3
- cameras: float32 [4, 6], replicated, may hold values from -0.004 to 0.004
- send_ids: int32 [128, 32, 256], P(('view', 'pix')), may hold values from -1 to 8191, as said below
- tile_lists: int32 [512, 2048], P('pix'), may hold values from -1 to 32767, as said below
- tile_perm: int32 [512], P('pix'), may hold values from 0 to 511, as said below
- targets: float32 [4, 512, 3, 256], P('view', 'pix'), may hold values from 0 to 1
Outputs:
- rendered: float32 [4, 512, 3, 256], P('view', 'pix')
- total_loss: float32 [], replicated
- grad_centers: float32 [3, 1048576], P(None, ('view', 'pix'))
- grad_scales: float32 [3, 1048576], P(None, ('view', 'pix'))
- grad_rotations: float32 [4, 1048576], P(None, ('view', 'pix'))
- grad_logits: float32 [1048576], P(('view', 'pix'))
- grad_harmonics: float32 [48, 1048576], P(None, ('view', 'pix'))
Inputs may be any that keep to these rules, and one draw needn't show every extreme that they name: `send_ids`: entry [s, p, c] is a local index of device s's Gaussians or -1; the indices of one device are distinct. `tile_lists`: in each row the listed receive slots come first, distinct, ordered front to back, then -1; a listed slot e of row r has send_ids[e // 256, r // 16, e % 256] >= 0 and (e % 256) // 16 == r % 16; some row has all 2048 entries. `tile_perm`: A permutation of the tiles of a view.
All inputs are finite; a program needn't handle non-finite values.
Results may differ from a plain program's by a relative error of at most 0.0003.
Values sent between devices are 32-bit elements; how exact they have to be, the bound alone decides.
A program may use at most 192 MiB of HBM per device.

v0:
```python
import jax
import jax.numpy as jnp
from jax import lax
from jax.sharding import PartitionSpec as P

TW = 16


FOCAL = 1100.0
BLUR = 0.3
SH_ZERO = 0.28209479177387814
SH_ONE = 0.4886025119029199
SH_TWO = (
    1.0925484305920792,
    -1.0925484305920792,
    0.31539156525252005,
    -1.0925484305920792,
    0.5462742152960396,
)
SH_THREE = (
    -0.5900435899266435,
    2.890611442640554,
    -0.4570457994644658,
    0.3731763325901154,
    -0.4570457994644658,
    1.445305721320277,
    -0.5900435899266435,
)
full_precision = lax.Precision.HIGHEST


def rotation_matrix(camera):
    cos_a, cos_b, cos_c = (jnp.cos(camera[0]), jnp.cos(camera[1]), jnp.cos(camera[2]))
    sin_a, sin_b, sin_c = (jnp.sin(camera[0]), jnp.sin(camera[1]), jnp.sin(camera[2]))
    return [
        [
            cos_c * cos_b,
            cos_c * sin_b * sin_a - sin_c * cos_a,
            cos_c * sin_b * cos_a + sin_c * sin_a,
        ],
        [
            sin_c * cos_b,
            sin_c * sin_b * sin_a + cos_c * cos_a,
            sin_c * sin_b * cos_a - cos_c * sin_a,
        ],
        [-sin_b, cos_b * sin_a, cos_b * cos_a],
    ]


def harmonics(direction):
    dir_x, dir_y, dir_z = (direction[0], direction[1], direction[2])
    sq_x, sq_y, sq_z = (dir_x * dir_x, dir_y * dir_y, dir_z * dir_z)
    terms = [
        SH_ZERO * jnp.ones_like(dir_x),
        -SH_ONE * dir_y,
        SH_ONE * dir_z,
        -SH_ONE * dir_x,
        SH_TWO[0] * dir_x * dir_y,
        SH_TWO[1] * dir_y * dir_z,
        SH_TWO[2] * (2.0 * sq_z - sq_x - sq_y),
        SH_TWO[3] * dir_x * dir_z,
        SH_TWO[4] * (sq_x - sq_y),
        SH_THREE[0] * dir_y * (3.0 * sq_x - sq_y),
        SH_THREE[1] * dir_x * dir_y * dir_z,
        SH_THREE[2] * dir_y * (4.0 * sq_z - sq_x - sq_y),
        SH_THREE[3] * dir_z * (2.0 * sq_z - 3.0 * sq_x - 3.0 * sq_y),
        SH_THREE[4] * dir_x * (4.0 * sq_z - sq_x - sq_y),
        SH_THREE[5] * dir_z * (sq_x - sq_y),
        SH_THREE[6] * dir_x * (sq_x - 3.0 * sq_y),
    ]
    return jnp.stack(terms)


def project(centers, log_scales, rotations, logits, harmonic_coeffs, camera, width_px, height_px):
    turn = rotation_matrix(camera)
    camera_pts = [
        sum((turn[line_idx][entry_idx] * centers[entry_idx] for entry_idx in range(3)))
        + camera[3 + line_idx]
        for line_idx in range(3)
    ]
    cam_x, cam_y, depth = camera_pts
    length_q = jnp.sqrt(jnp.sum(rotations * rotations, axis=0))
    unit = rotations / length_q[None, :]
    scalar_part, vector_x, vector_y, vector_z = (unit[0], unit[1], unit[2], unit[3])
    quat_turn = [
        [
            1.0 - 2.0 * (vector_y * vector_y + vector_z * vector_z),
            2.0 * (vector_x * vector_y - scalar_part * vector_z),
            2.0 * (vector_x * vector_z + scalar_part * vector_y),
        ],
        [
            2.0 * (vector_x * vector_y + scalar_part * vector_z),
            1.0 - 2.0 * (vector_x * vector_x + vector_z * vector_z),
            2.0 * (vector_y * vector_z - scalar_part * vector_x),
        ],
        [
            2.0 * (vector_x * vector_z - scalar_part * vector_y),
            2.0 * (vector_y * vector_z + scalar_part * vector_x),
            1.0 - 2.0 * (vector_x * vector_x + vector_y * vector_y),
        ],
    ]
    spread = jnp.exp(log_scales)
    shaped = [
        [quat_turn[line_idx][entry_idx] * spread[entry_idx] for entry_idx in range(3)]
        for line_idx in range(3)
    ]
    sigma = [
        [
            sum(
                (
                    shaped[line_idx][inner_idx] * shaped[entry_idx][inner_idx]
                    for inner_idx in range(3)
                )
            )
            for entry_idx in range(3)
        ]
        for line_idx in range(3)
    ]
    inverse_depth = 1.0 / depth
    jac_diag = FOCAL * inverse_depth
    jac_x = -FOCAL * cam_x * inverse_depth * inverse_depth
    jac_y = -FOCAL * cam_y * inverse_depth * inverse_depth
    first_row = [
        jac_diag * turn[0][entry_idx] + jac_x * turn[2][entry_idx] for entry_idx in range(3)
    ]
    second_row = [
        jac_diag * turn[1][entry_idx] + jac_y * turn[2][entry_idx] for entry_idx in range(3)
    ]

    def quadratic(left_row, right_row):
        return sum(
            (
                left_row[line_idx] * sigma[line_idx][entry_idx] * right_row[entry_idx]
                for line_idx in range(3)
                for entry_idx in range(3)
            )
        )

    cov_xx = quadratic(first_row, first_row) + BLUR
    cov_xy = quadratic(first_row, second_row)
    cov_yy = quadratic(second_row, second_row) + BLUR
    determinant = cov_xx * cov_yy - cov_xy * cov_xy
    screen_x = FOCAL * cam_x * inverse_depth + 0.5 * width_px
    screen_y = FOCAL * cam_y * inverse_depth + 0.5 * height_px
    opacity = jax.nn.sigmoid(logits)
    anchor = [
        -sum((turn[line_idx][entry_idx] * camera[3 + line_idx] for line_idx in range(3)))
        for entry_idx in range(3)
    ]
    offsets = jnp.stack([centers[entry_idx] - anchor[entry_idx] for entry_idx in range(3)])
    direction = offsets / jnp.sqrt(jnp.sum(offsets * offsets, axis=0))[None, :]
    basis = harmonics(direction)
    colour = jnp.maximum(
        jnp.sum(harmonic_coeffs.reshape(3, 16, -1) * basis[None], axis=1) + 0.5, 0.0
    )
    return jnp.stack(
        [
            screen_x,
            screen_y,
            cov_yy / determinant,
            -cov_xy / determinant,
            cov_xx / determinant,
            opacity,
            colour[0],
            colour[1],
            colour[2],
        ]
    )


def alpha_of(record, pixel_x, pixel_y):
    delta_x = pixel_x[:, None] - record[0][None, :]
    delta_y = pixel_y[:, None] - record[1][None, :]
    exponent = (
        -0.5 * (record[2][None, :] * delta_x * delta_x + record[4][None, :] * delta_y * delta_y)
        - record[3][None, :] * delta_x * delta_y
    )
    return record[5][None, :] * jnp.exp(exponent)


def local(
    centers,
    log_scales,
    rotations,
    logits,
    harmonic_coeffs,
    cameras,
    send_ids,
    tile_lists,
    tile_perm,
    targets,
):
    view_count = lax.axis_size("view")
    pix_count = lax.axis_size("pix")
    device_count = view_count * pix_count
    tiles_local = tile_perm.shape[0]
    tile_total = tiles_local * pix_count
    width_px = 16 * TW
    height_px = 16 * (tile_total // TW)
    capacity = send_ids.shape[2]
    per_slot = capacity // tiles_local
    slot_ids = send_ids[0].reshape(-1)
    present_mask = (slot_ids >= 0).astype(jnp.float32)
    safe_ids = jnp.where(slot_ids >= 0, slot_ids, 0)

    def outgoing(params):
        picked = [jnp.take(param, safe_ids, axis=-1) for param in params]
        blocks = []
        for view_idx in range(view_count):
            record = project(
                picked[0],
                picked[1],
                picked[2],
                picked[3],
                picked[4],
                cameras[view_idx],
                width_px,
                height_px,
            )
            blocks.append(record * present_mask[None, :])
        return jnp.stack(blocks, axis=1)

    sending, pullback = jax.vjp(outgoing, (centers, log_scales, rotations, logits, harmonic_coeffs))
    received = lax.all_to_all(
        sending.reshape(9, device_count * capacity),
        ("view", "pix"),
        split_axis=1,
        concat_axis=1,
        tiled=True,
    )
    received_slots = received.reshape(9, device_count, tiles_local, per_slot)
    list_size = tile_lists.shape[1]
    block = min(256, list_size)
    block_count = list_size // block
    offsets = jnp.arange(256, dtype=jnp.int32)
    column_off = offsets % 16
    row_off = offsets // 16

    def tile_work(packed):
        entry, place, target, slot_local = packed
        valid = entry >= 0
        valid_mask = valid.astype(jnp.float32)
        candidates = lax.dynamic_index_in_dim(
            received_slots, slot_local, 2, keepdims=False
        ).reshape(9, list_size)
        column = entry // capacity * per_slot + entry % per_slot
        safe_column = jnp.where(valid, column, 0)
        drop_column = jnp.where(valid, column, list_size)
        ordered = jnp.take(candidates, safe_column, axis=1) * valid_mask[None, :]
        pixel_x = (16 * (place % TW) + column_off).astype(jnp.float32)
        pixel_y = (16 * (place // TW) + row_off).astype(jnp.float32)

        def first_pass(block_idx, carry):
            prefix, colour, stored = carry
            piece = lax.dynamic_slice_in_dim(ordered, block_idx * block, block, 1)
            alphas = alpha_of(piece, pixel_x, pixel_y)
            log_keep = jnp.log(1.0 - alphas)
            inclusive = jnp.cumsum(log_keep, axis=1)
            transmit = jnp.exp(prefix[:, None] + inclusive - log_keep)
            weights = alphas * transmit
            colour = colour + jnp.dot(piece[6:9], weights.T, precision=full_precision)
            stored = lax.dynamic_update_index_in_dim(stored, transmit, block_idx, 0)
            return (prefix + inclusive[:, -1], colour, stored)

        start_prefix = jnp.zeros((256,), jnp.float32)
        kept = jnp.zeros((block_count, 256, block), jnp.float32)
        _, colour, kept = lax.fori_loop(
            0, block_count, first_pass, (start_prefix, jnp.zeros((3, 256), jnp.float32), kept)
        )
        residual = colour - target
        total_shade = jnp.sum(residual * colour, axis=0)

        def second_pass(block_idx, carry):
            partial_sum, grads = carry
            piece = lax.dynamic_slice_in_dim(ordered, block_idx * block, block, 1)
            transmit = lax.dynamic_index_in_dim(kept, block_idx, 0, keepdims=False)
            alphas, alpha_pull = jax.vjp(lambda chosen: alpha_of(chosen, pixel_x, pixel_y), piece)
            weights = alphas * transmit
            shade = jnp.dot(residual.T, piece[6:9], precision=full_precision)
            shaded = shade * weights
            upto_sum = partial_sum[:, None] + jnp.cumsum(shaded, axis=1)
            d_alpha = shade * transmit - (total_shade[:, None] - upto_sum) / (1.0 - alphas)
            (d_piece,) = alpha_pull(d_alpha)
            d_colour = jnp.dot(residual, weights, precision=full_precision)
            d_piece = d_piece.at[6:9].set(d_colour)
            grads = lax.dynamic_update_slice_in_dim(grads, d_piece, block_idx * block, 1)
            return (upto_sum[:, -1], grads)

        _, d_ordered = lax.fori_loop(
            0,
            block_count,
            second_pass,
            (jnp.zeros((256,), jnp.float32), jnp.zeros((9, list_size), jnp.float32)),
        )
        d_candidates = (
            jnp.zeros((9, list_size), jnp.float32).at[:, drop_column].add(d_ordered, mode="drop")
        )
        return (colour, d_candidates, 0.5 * jnp.sum(residual * residual))

    slot_numbers = jnp.arange(tiles_local, dtype=jnp.int32)
    colours, d_candidates, tile_losses = lax.map(
        tile_work, (tile_lists, tile_perm, targets[0], slot_numbers)
    )
    d_received = jnp.transpose(
        d_candidates.reshape(tiles_local, 9, device_count, per_slot), (1, 2, 0, 3)
    ).reshape(9, device_count * capacity)
    returned = lax.all_to_all(
        d_received, ("view", "pix"), split_axis=1, concat_axis=1, tiled=True
    ).reshape(sending.shape)
    (grads,) = pullback(returned)
    total_loss = lax.psum(jnp.sum(tile_losses), ("view", "pix"))
    return (colours[None], total_loss, grads[0], grads[1], grads[2], grads[3], grads[4])


def solution(mesh):
    return jax.shard_map(
        local,
        mesh=mesh,
        in_specs=(
            P(None, ("view", "pix")),
            P(None, ("view", "pix")),
            P(None, ("view", "pix")),
            P(("view", "pix")),
            P(None, ("view", "pix")),
            P(),
            P(("view", "pix"), None, None),
            P("pix", None),
            P("pix"),
            P("view", "pix", None, None),
        ),
        out_specs=(
            P("view", "pix", None, None),
            P(),
            P(None, ("view", "pix")),
            P(None, ("view", "pix")),
            P(None, ("view", "pix")),
            P(("view", "pix")),
            P(None, ("view", "pix")),
        ),
        check_vma=False,
    )
```

profile of v0, /device:TPU:25, one launch (start us, length us, event | category | flops | bytes accessed | tf_op | source)
XLA Modules:
  0.0 2437.5 jit_solution(2597364002334544295)
XLA Ops:
  46.5 30.1 %gather_fusion.4 = f32[8192,3]{1,0:T(8,128)} fusion(f32[3,8192]{0,1:T(8,128)} %copy.1302, s32[8192]{0:T(1024)S(1)} %get-tuple-element.1544), kind=kCustom, calls=%fused_computation.clone | custom fusion | bytes 229376 | tf_op jit(solution)/shard_map/jvp(jit(_take))/gather | solution.py:207
  106.7 30.1 %gather_fusion.5 = f32[8192,3]{1,0:T(8,128)} fusion(f32[3,8192]{0,1:T(8,128)} %copy.1306, s32[8192]{0:T(1024)S(1)} %get-tuple-element.1544), kind=kCustom, calls=%fused_computation.2.clone | custom fusion | bytes 229376 | tf_op jit(solution)/shard_map/jvp(jit(_take))/gather | solution.py:207
  142.5 80.4 %gather_fusion.2 = f32[8192]{0:T(1024)} fusion(f32[8192]{0:T(1024)S(1)} %copy-done, s32[8192]{0:T(1024)S(1)} %get-tuple-element.1578), kind=kCustom, calls=%fused_computation.4 | custom fusion | bytes 98304 | tf_op jit(solution)/shard_map/jvp(jit(_take))/gather | solution.py:207
  222.9 30.1 %gather_fusion.1 = f32[8192,4]{1,0:T(8,128)} fusion(f32[4,8192]{0,1:T(8,128)} %copy.1304, s32[8192]{0:T(1024)S(1)} %get-tuple-element.1578), kind=kCustom, calls=%fused_computation.3 | custom fusion | bytes 294912 | tf_op jit(solution)/shard_map/jvp(jit(_take))/gather | solution.py:207
  259.5 30.1 %gather_fusion.3 = f32[8192,48]{1,0:T(8,128)} fusion(f32[48,8192]{0,1:T(8,128)} %copy.1308, s32[8192]{0:T(1024)S(1)} %get-tuple-element.1578), kind=kCustom, calls=%fused_computation.5 | custom fusion | bytes 3178496 | tf_op jit(solution)/shard_map/jvp(jit(_take))/gather | solution.py:207
  289.6 15.2 copy.1309
  339.7 11.1 all-to-all-start
  351.5 27.7 %all-to-all-done = f32[9,128,256]{2,0,1:T(8,128)S(1)} async-done(((f32[9,128,256]{2,0,1:T(8,128)}), f32[9,128,256]{2,0,1:T(8,128)S(1)}, u32[]{:S(2)}, u32[]{:S(2)}) %all-to-all-start) | async-done | bytes 1179680 | tf_op jit(solution)/shard_map/all_to_all | solution.py:224
  380.7 1593.8 %while.77 = (s32[]{:T(128)}, f32[16,3,256]{2,0,1:T(8,128)}, f32[16,9,2048]{1,2,0:T(8,128)}, f32[16]{0:T(128)}, s32[16,2048]{1,0:T(8,128)}, /*index=5*/s32[16]{0:...) while((s32[]{:T(128)}, f32[16,3,256]{2,0,1:T(8,128)}, ...), condition=%wide.region_27.29_spmd.clone, body=%wide.region_9.28_spmd.clone.sunk | while | flops 32400688 | bytes 9375767 | solution.py:301
  396.0 21.3 while.78
  422.6 43.1 %while.79 = (s32[]{:T(128)}, f32[256]{0:T(256)}, f32[9,2048]{1,0:T(8,128)S(1)}, f32[9,2048]{1,0:T(8,128)S(1)}, f32[3,256]{1,0:T(4,128)}, /*index=5*/f32[256]{0:T...) while((s32[]{:T(128)}, f32[256]{0:T(256)}, ...), condition=%wide.region_24.25_spmd, body=%wide.region_15.24_spmd.sunk | while | flops 18557964 | bytes 4876659 | solution.py:289
  467.4 11.8 scatter_custom_fusion.16
  495.6 21.3 while.78
  522.2 43.1 %while.79 = (s32[]{:T(128)}, f32[256]{0:T(256)}, f32[9,2048]{1,0:T(8,128)S(1)}, f32[9,2048]{1,0:T(8,128)S(1)}, f32[3,256]{1,0:T(4,128)}, /*index=5*/f32[256]{0:T...) while((s32[]{:T(128)}, f32[256]{0:T(256)}, ...), condition=%wide.region_24.25_spmd, body=%wide.region_15.24_spmd.sunk | while | flops 18557964 | bytes 4876659 | solution.py:289
  567.0 11.8 scatter_custom_fusion.16
  595.2 21.3 while.78
  621.8 43.1 %while.79 = (s32[]{:T(128)}, f32[256]{0:T(256)}, f32[9,2048]{1,0:T(8,128)S(1)}, f32[9,2048]{1,0:T(8,128)S(1)}, f32[3,256]{1,0:T(4,128)}, /*index=5*/f32[256]{0:T...) while((s32[]{:T(128)}, f32[256]{0:T(256)}, ...), condition=%wide.region_24.25_spmd, body=%wide.region_15.24_spmd.sunk | while | flops 18557964 | bytes 4876659 | solution.py:289
  666.6 11.8 scatter_custom_fusion.16
  694.9 21.3 while.78
  721.4 43.1 %while.79 = (s32[]{:T(128)}, f32[256]{0:T(256)}, f32[9,2048]{1,0:T(8,128)S(1)}, f32[9,2048]{1,0:T(8,128)S(1)}, f32[3,256]{1,0:T(4,128)}, /*index=5*/f32[256]{0:T...) while((s32[]{:T(128)}, f32[256]{0:T(256)}, ...), condition=%wide.region_24.25_spmd, body=%wide.region_15.24_spmd.sunk | while | flops 18557964 | bytes 4876659 | solution.py:289
  766.3 11.8 scatter_custom_fusion.16
  794.5 21.3 while.78
  821.0 43.1 %while.79 = (s32[]{:T(128)}, f32[256]{0:T(256)}, f32[9,2048]{1,0:T(8,128)S(1)}, f32[9,2048]{1,0:T(8,128)S(1)}, f32[3,256]{1,0:T(4,128)}, /*index=5*/f32[256]{0:T...) while((s32[]{:T(128)}, f32[256]{0:T(256)}, ...), condition=%wide.region_24.25_spmd, body=%wide.region_15.24_spmd.sunk | while | flops 18557964 | bytes 4876659 | solution.py:289
  865.9 11.8 scatter_custom_fusion.16
  894.1 21.3 while.78
  920.6 43.1 %while.79 = (s32[]{:T(128)}, f32[256]{0:T(256)}, f32[9,2048]{1,0:T(8,128)S(1)}, f32[9,2048]{1,0:T(8,128)S(1)}, f32[3,256]{1,0:T(4,128)}, /*index=5*/f32[256]{0:T...) while((s32[]{:T(128)}, f32[256]{0:T(256)}, ...), condition=%wide.region_24.25_spmd, body=%wide.region_15.24_spmd.sunk | while | flops 18557964 | bytes 4876659 | solution.py:289
  965.5 11.8 scatter_custom_fusion.16
  993.6 21.3 while.78
  1020.2 43.1 %while.79 = (s32[]{:T(128)}, f32[256]{0:T(256)}, f32[9,2048]{1,0:T(8,128)S(1)}, f32[9,2048]{1,0:T(8,128)S(1)}, f32[3,256]{1,0:T(4,128)}, /*index=5*/f32[256]{0:T...) while((s32[]{:T(128)}, f32[256]{0:T(256)}, ...), condition=%wide.region_24.25_spmd, body=%wide.region_15.24_spmd.sunk | while | flops 18557964 | bytes 4876659 | solution.py:289
  1065.0 11.8 scatter_custom_fusion.16
  1093.3 21.3 while.78
  1119.8 43.1 %while.79 = (s32[]{:T(128)}, f32[256]{0:T(256)}, f32[9,2048]{1,0:T(8,128)S(1)}, f32[9,2048]{1,0:T(8,128)S(1)}, f32[3,256]{1,0:T(4,128)}, /*index=5*/f32[256]{0:T...) while((s32[]{:T(128)}, f32[256]{0:T(256)}, ...), condition=%wide.region_24.25_spmd, body=%wide.region_15.24_spmd.sunk | while | flops 18557964 | bytes 4876659 | solution.py:289
  1164.7 11.8 scatter_custom_fusion.16
  1192.9 21.3 while.78
  1219.4 43.1 %while.79 = (s32[]{:T(128)}, f32[256]{0:T(256)}, f32[9,2048]{1,0:T(8,128)S(1)}, f32[9,2048]{1,0:T(8,128)S(1)}, f32[3,256]{1,0:T(4,128)}, /*index=5*/f32[256]{0:T...) while((s32[]{:T(128)}, f32[256]{0:T(256)}, ...), condition=%wide.region_24.25_spmd, body=%wide.region_15.24_spmd.sunk | while | flops 18557964 | bytes 4876659 | solution.py:289
  1264.3 11.8 scatter_custom_fusion.16
  1292.5 21.3 while.78
  1319.0 43.1 %while.79 = (s32[]{:T(128)}, f32[256]{0:T(256)}, f32[9,2048]{1,0:T(8,128)S(1)}, f32[9,2048]{1,0:T(8,128)S(1)}, f32[3,256]{1,0:T(4,128)}, /*index=5*/f32[256]{0:T...) while((s32[]{:T(128)}, f32[256]{0:T(256)}, ...), condition=%wide.region_24.25_spmd, body=%wide.region_15.24_spmd.sunk | while | flops 18557964 | bytes 4876659 | solution.py:289
  1363.9 11.8 scatter_custom_fusion.16
  1392.1 21.3 while.78
  1418.7 43.1 %while.79 = (s32[]{:T(128)}, f32[256]{0:T(256)}, f32[9,2048]{1,0:T(8,128)S(1)}, f32[9,2048]{1,0:T(8,128)S(1)}, f32[3,256]{1,0:T(4,128)}, /*index=5*/f32[256]{0:T...) while((s32[]{:T(128)}, f32[256]{0:T(256)}, ...), condition=%wide.region_24.25_spmd, body=%wide.region_15.24_spmd.sunk | while | flops 18557964 | bytes 4876659 | solution.py:289
  1463.5 11.8 scatter_custom_fusion.16
  1491.8 21.3 while.78
  1518.3 43.1 %while.79 = (s32[]{:T(128)}, f32[256]{0:T(256)}, f32[9,2048]{1,0:T(8,128)S(1)}, f32[9,2048]{1,0:T(8,128)S(1)}, f32[3,256]{1,0:T(4,128)}, /*index=5*/f32[256]{0:T...) while((s32[]{:T(128)}, f32[256]{0:T(256)}, ...), condition=%wide.region_24.25_spmd, body=%wide.region_15.24_spmd.sunk | while | flops 18557964 | bytes 4876659 | solution.py:289
  1563.2 11.8 scatter_custom_fusion.16
  1591.4 21.3 while.78
  1617.9 43.1 %while.79 = (s32[]{:T(128)}, f32[256]{0:T(256)}, f32[9,2048]{1,0:T(8,128)S(1)}, f32[9,2048]{1,0:T(8,128)S(1)}, f32[3,256]{1,0:T(4,128)}, /*index=5*/f32[256]{0:T...) while((s32[]{:T(128)}, f32[256]{0:T(256)}, ...), condition=%wide.region_24.25_spmd, body=%wide.region_15.24_spmd.sunk | while | flops 18557964 | bytes 4876659 | solution.py:289
  1662.8 11.8 scatter_custom_fusion.16
  1691.0 21.3 while.78
  1717.5 43.1 %while.79 = (s32[]{:T(128)}, f32[256]{0:T(256)}, f32[9,2048]{1,0:T(8,128)S(1)}, f32[9,2048]{1,0:T(8,128)S(1)}, f32[3,256]{1,0:T(4,128)}, /*index=5*/f32[256]{0:T...) while((s32[]{:T(128)}, f32[256]{0:T(256)}, ...), condition=%wide.region_24.25_spmd, body=%wide.region_15.24_spmd.sunk | while | flops 18557964 | bytes 4876659 | solution.py:289
  1762.4 11.8 scatter_custom_fusion.16
  1790.6 21.3 while.78
  1817.1 43.1 %while.79 = (s32[]{:T(128)}, f32[256]{0:T(256)}, f32[9,2048]{1,0:T(8,128)S(1)}, f32[9,2048]{1,0:T(8,128)S(1)}, f32[3,256]{1,0:T(4,128)}, /*index=5*/f32[256]{0:T...) while((s32[]{:T(128)}, f32[256]{0:T(256)}, ...), condition=%wide.region_24.25_spmd, body=%wide.region_15.24_spmd.sunk | while | flops 18557964 | bytes 4876659 | solution.py:289
  1862.0 11.8 scatter_custom_fusion.16
  1890.2 21.3 while.78
  1916.7 43.1 %while.79 = (s32[]{:T(128)}, f32[256]{0:T(256)}, f32[9,2048]{1,0:T(8,128)S(1)}, f32[9,2048]{1,0:T(8,128)S(1)}, f32[3,256]{1,0:T(4,128)}, /*index=5*/f32[256]{0:T...) while((s32[]{:T(128)}, f32[256]{0:T(256)}, ...), condition=%wide.region_24.25_spmd, body=%wide.region_15.24_spmd.sunk | while | flops 18557964 | bytes 4876659 | solution.py:289
  1961.6 11.8 scatter_custom_fusion.16
  1974.5 10.8 copy.1320
  1994.7 80.5 %psum.7 = f32[]{:T(128)} all-reduce(f32[]{:T(128)} %reduce_sum.425), channel_id=1, replica_groups=mesh['view'=4,'pix'=32] {'view','pix'}, use_global_device_ids=true, to_apply=%region_29.31 | all-reduce | flops 1 | bytes 8 | tf_op jit(solution)/shard_map/psum | solution.py:311
  2106.1 46.1 %scatter_custom_fusion.4 = f32[8192]{0:T(1024)} fusion(s32[8192]{0:T(1024)} %bitcast.512, f32[8192]{0:T(1024)S(1)} %fusion.156, f32[]{:T(128)} %constant.491.clone.1), kind=kCustom, calls=%fused_computation.873 | custom fusion | flops 8192 | bytes 33280 | tf_op jit(solution)/shard_map/transpose(jvp(jit(_take)))/scatter-add | solution.py:207
  2212.6 47.7 %scatter_custom_fusion.5 = f32[48,8192]{0,1:T(8,128)} fusion(s32[8192]{0:T(1024)} %bitcast.513, f32[8192,48]{1,0:T(8,128)} %copy.1332, f32[]{:T(128)} %constant.491.clone.1), kind=kCustom, calls=%fused_computation.192 | custom fusion | flops 393216 | bytes 1573376 | tf_op jit(solution)/shard_map/transpose(jvp(jit(_take)))/scatter-add | solution.py:207
  2269.3 47.5 %scatter_custom_fusion.3 = f32[4,8192]{0,1:T(8,128)} fusion(s32[8192]{0:T(1024)} %bitcast.514, f32[8192,4]{1,0:T(8,128)} %copy.1331, f32[]{:T(128)} %constant.491.clone.1), kind=kCustom, calls=%fused_computation.194 | custom fusion | flops 32768 | bytes 131584 | tf_op jit(solution)/shard_map/transpose(jvp(jit(_take)))/scatter-add | solution.py:207
  2327.3 47.7 %scatter_custom_fusion.1 = f32[3,8192]{0,1:T(8,128)} fusion(s32[8192]{0:T(1024)} %get-tuple-element.1543, f32[8192,3]{1,0:T(8,128)} %copy.1328, f32[]{:T(128)} %constant.491.clone.1), kind=kCustom, calls=%fused_computation.190 | custom fusion | flops 24576 | bytes 98816 | tf_op jit(solution)/shard_map/transpose(jvp(jit(_take)))/scatter-add | solution.py:207
  2386.1 47.5 %scatter_custom_fusion.2 = f32[3,8192]{0,1:T(8,128)} fusion(s32[8192]{0:T(1024)} %get-tuple-element.1543, f32[8192,3]{1,0:T(8,128)} %copy.1330, f32[]{:T(128)} %constant.491.clone.1), kind=kCustom, calls=%fused_computation.188 | custom fusion | flops 24576 | bytes 98816 | tf_op jit(solution)/shard_map/transpose(jvp(jit(_take)))/scatter-add | solution.py:207
  (6042 shorter events, 1514.7 us)
Async XLA Ops:
  0.6 141.8 %copy-start = (f32[8192]{0:T(1024)S(1)}, f32[8192]{0:T(1024)}, u32[]{:S(2)}) copy-start(f32[8192]{0:T(1024)} %param.23) | copy-start | bytes 98308
  42.4 273.9 %copy-start.71 = (pred[8192]{0:T(1024)(128)(4,1)}, pred[8192]{0:T(1024)(128)(4,1)S(1)}, u32[]{:S(2)}) copy-start(pred[8192]{0:T(1024)(128)(4,1)S(1)} %get-tuple-element.1553) | copy-start | bytes 24580
  88.0 231.1 %copy-start.78 = (f32[1,8192]{1,0:T(1,128)}, f32[1,8192]{1,0:T(1,128)S(1)}, u32[]{:S(2)}) copy-start(f32[1,8192]{1,0:T(1,128)S(1)} %get-tuple-element.1241) | copy-start | bytes 98308
  92.0 227.2 %copy-start.76 = (f32[1,8192]{1,0:T(1,128)}, f32[1,8192]{1,0:T(1,128)S(1)}, u32[]{:S(2)}) copy-start(f32[1,8192]{1,0:T(1,128)S(1)} %get-tuple-element.1208) | copy-start | bytes 98308
  289.6 15.3 copy-start.346
  289.6 15.4 copy-start.347
  289.6 15.4 copy-start.348
  289.6 15.4 copy-start.349
  289.6 15.4 copy-start.350
  289.6 16.2 copy-start.340
  289.6 16.2 copy-start.341
  289.6 16.2 copy-start.342
  289.6 16.2 copy-start.343
  339.7 39.6 %all-to-all-start = ((f32[9,128,256]{2,0,1:T(8,128)}), f32[9,128,256]{2,0,1:T(8,128)S(1)}, u32[]{:S(2)}, u32[]{:S(2)}) async-start(f32[9,128,256]{2,0,1:T(8,128)} %copy.1314), calls=%async_computation | async-start | bytes 4194304 | tf_op jit(solution)/shard_map/all_to_all | solution.py:224
  350.8 29.9 %copy-start.378 = (s32[16]{0:T(128)S(1)}, s32[16]{0:T(128)}, u32[]{:S(2)}) copy-start(s32[16]{0:T(128)} %param.28) | copy-start | bytes 196
  467.1 13.3 copy-start.379
  467.1 13.3 copy-start.381
  566.7 13.3 copy-start.379
  566.7 13.3 copy-start.381
  666.3 13.3 copy-start.379
  666.3 13.3 copy-start.381
  765.9 13.3 copy-start.379
  765.9 13.3 copy-start.381
  865.5 13.3 copy-start.379
  865.5 13.3 copy-start.381
  965.1 13.2 copy-start.381
  1064.7 13.3 copy-start.379
  1064.7 13.3 copy-start.381
  1164.3 13.3 copy-start.379
  1164.3 13.3 copy-start.381
  1263.9 13.3 copy-start.379
  1263.9 13.3 copy-start.381
  1363.5 13.3 copy-start.379
  1363.5 13.3 copy-start.381
  1463.2 13.3 copy-start.379
  1463.2 13.3 copy-start.381
  1562.8 13.3 copy-start.379
  1562.8 13.3 copy-start.381
  1662.4 13.3 copy-start.379
  1662.4 13.3 copy-start.381
  1762.0 13.3 copy-start.379
  1762.0 13.3 copy-start.381
  1861.6 13.3 copy-start.379
  1861.6 13.3 copy-start.381
  1961.2 13.3 copy-start.379
  1961.2 13.3 copy-start.381
  1987.3 87.9 %all-to-all-start.1 = ((f32[9,128,256]{2,0,1:T(8,128)}), f32[9,128,256]{2,0,1:T(8,128)S(1)}, u32[]{:S(2)}, u32[]{:S(2)}) async-start(f32[9,128,256]{2,0,1:T(8,128)} %copy.1321), calls=%async_computation.1 | async-start | bytes 4194304 | tf_op jit(solution)/shard_map/all_to_all | solution.py:307
  2104.7 54.2 %copy-start.20 = (f32[1,8192]{1,0:T(1,128)S(1)}, f32[1,8192]{1,0:T(1,128)}, u32[]{:S(2)}) copy-start(f32[1,8192]{1,0:T(1,128)} %copy-done.18) | copy-start | bytes 98308
  2104.7 54.2 %copy-start.23 = (f32[1,8192]{1,0:T(1,128)S(1)}, f32[1,8192]{1,0:T(1,128)}, u32[]{:S(2)}) copy-start(f32[1,8192]{1,0:T(1,128)} %copy-done.21) | copy-start | bytes 98308
  2104.8 54.2 %copy-start.26 = (f32[1,8192]{1,0:T(1,128)S(1)}, f32[1,8192]{1,0:T(1,128)}, u32[]{:S(2)}) copy-start(f32[1,8192]{1,0:T(1,128)} %copy-done.24) | copy-start | bytes 98308
  2104.8 54.2 %copy-start.29 = (f32[1,8192]{1,0:T(1,128)S(1)}, f32[1,8192]{1,0:T(1,128)}, u32[]{:S(2)}) copy-start(f32[1,8192]{1,0:T(1,128)} %copy-done.27) | copy-start | bytes 98308
  2104.8 54.2 %copy-start.32 = (f32[1,8192]{1,0:T(1,128)S(1)}, f32[1,8192]{1,0:T(1,128)}, u32[]{:S(2)}) copy-start(f32[1,8192]{1,0:T(1,128)} %copy-done.30) | copy-start | bytes 98308
  2104.8 54.2 %copy-start.84 = (f32[1,8192]{1,0:T(1,128)S(1)}, f32[1,8192]{1,0:T(1,128)}, u32[]{:S(2)}) copy-start(f32[1,8192]{1,0:T(1,128)} %get-tuple-element.1315) | copy-start | bytes 98308
  2104.8 54.2 %copy-start.89 = (f32[1,8192]{1,0:T(1,128)S(1)}, f32[1,8192]{1,0:T(1,128)}, u32[]{:S(2)}) copy-start(f32[1,8192]{1,0:T(1,128)} %get-tuple-element.1307) | copy-start | bytes 98308
  2104.8 54.2 %copy-start.178 = (f32[1,8192]{1,0:T(1,128)S(1)}, f32[1,8192]{1,0:T(1,128)}, u32[]{:S(2)}) copy-start(f32[1,8192]{1,0:T(1,128)} %get-tuple-element.1314) | copy-start | bytes 98308
  2104.8 54.2 %copy-start.187 = (f32[1,8192]{1,0:T(1,128)S(1)}, f32[1,8192]{1,0:T(1,128)}, u32[]{:S(2)}) copy-start(f32[1,8192]{1,0:T(1,128)} %copy-done.186) | copy-start | bytes 98308
  2104.8 54.2 %copy-start.209 = (f32[1,8192]{1,0:T(1,128)S(1)}, f32[1,8192]{1,0:T(1,128)}, u32[]{:S(2)}) copy-start(f32[1,8192]{1,0:T(1,128)} %get-tuple-element.1310) | copy-start | bytes 98308
  2104.8 54.2 %copy-start.286 = (f32[1,8192]{1,0:T(1,128)S(1)}, f32[1,8192]{1,0:T(1,128)}, u32[]{:S(2)}) copy-start(f32[1,8192]{1,0:T(1,128)} %get-tuple-element.1316) | copy-start | bytes 98308
  2104.8 54.2 %copy-start.305 = (f32[1,8192]{1,0:T(1,128)S(1)}, f32[1,8192]{1,0:T(1,128)}, u32[]{:S(2)}) copy-start(f32[1,8192]{1,0:T(1,128)} %get-tuple-element.1288) | copy-start | bytes 98308
  2104.8 54.2 %copy-start.306 = (f32[1,8192]{1,0:T(1,128)S(1)}, f32[1,8192]{1,0:T(1,128)}, u32[]{:S(2)}) copy-start(f32[1,8192]{1,0:T(1,128)} %get-tuple-element.1289) | copy-start | bytes 98308
  2104.9 54.2 %copy-start.307 = (f32[1,8192]{1,0:T(1,128)S(1)}, f32[1,8192]{1,0:T(1,128)}, u32[]{:S(2)}) copy-start(f32[1,8192]{1,0:T(1,128)} %get-tuple-element.1290) | copy-start | bytes 98308
  2171.4 13.7 copy-start.114
  2198.4 65.8 %copy-start.226 = (f32[1,8192]{1,0:T(1,128)}, f32[1,8192]{1,0:T(1,128)S(1)}, u32[]{:S(2)}) copy-start(f32[1,8192]{1,0:T(1,128)S(1)} %get-tuple-element.1007) | copy-start | bytes 98308
  2386.1 51.0 %copy-start.1 = (f32[8192]{0:T(1024)S(1)}, f32[8192]{0:T(1024)}, u32[]{:S(2)}) copy-start(f32[8192]{0:T(1024)} %param.23) | copy-start | bytes 98308
  (366 other events, 2290.4 us)
where the time goes:
time: 2470 us; the launch traced here: 2440 us
  other arithmetic  1030 us (42%)
  local copies, waits for them, and re-layouts  746 us (30%)
  matrix products  381 us (15%)
  loops' own time  104 us (4%)
  blocking collectives  80.5 us (3%)
  between operations  46.6 us (2%)
  waiting for transfers between devices  27.7 us (1%)
    scatter-add x5, other arithmetic, outgoing(): picked = [jnp.take(param, safe_ids, axis=-1) for param in params]  237 us
    gather x9, local copies, waits for them, and re-layouts, outgoing(): picked = [jnp.take(param, safe_ids, axis=-1) for param in params]  225 us
    scatter-add x16, other arithmetic, tile_work(): jnp.zeros((9, list_size), jnp.float32).at[:, drop_column]  189 us
    dot_general x128, matrix products, second_pass(): shade = jnp.dot(residual.T, piece[6:9], precision=full_precision)  170 us
    another operation x785, other arithmetic  157 us
    dot_general x128, matrix products, second_pass(): d_colour = jnp.dot(residual, weights, precision=full_precision)  147 us
    mul x128, other arithmetic, alpha_of(): return record[5][None, :] * jnp.exp(exponent)  126 us
    gather x16, local copies, waits for them, and re-layouts, tile_work(): ordered = jnp.take(candidates, safe_column, axis=1) * valid_mask[None, :]  87.4 us

commit v1 on v0

v1 whole, which is shorter than its diff:
```python
import functools

import jax
import jax.numpy as jnp
from jax import lax
from jax.experimental import pallas as pl
from jax.experimental.pallas import tpu as pltpu
from jax.sharding import PartitionSpec as P

TW = 16
FOCAL = 1100.0
BLUR = 0.3
SH_ZERO = 0.28209479177387814
SH_ONE = 0.4886025119029199
SH_TWO = (
    1.0925484305920792,
    -1.0925484305920792,
    0.31539156525252005,
    -1.0925484305920792,
    0.5462742152960396,
)
SH_THREE = (
    -0.5900435899266435,
    2.890611442640554,
    -0.4570457994644658,
    0.3731763325901154,
    -0.4570457994644658,
    1.445305721320277,
    -0.5900435899266435,
)
LOG2E = 1.4426950408889634
LANES = 128
VIEWS = 4
FIELDS = 9
MSG = 24
TBL = 40
BLOCKS = 64
F32 = jnp.float32
I32 = jnp.int32
BF16 = jnp.bfloat16


def camera_numbers(cameras):
    cos, sin = jnp.cos(cameras[:, :3]), jnp.sin(cameras[:, :3])
    ca, cb, cc = cos[:, 0], cos[:, 1], cos[:, 2]
    sa, sb, sc = sin[:, 0], sin[:, 1], sin[:, 2]
    turn = [
        [cc * cb, cc * sb * sa - sc * ca, cc * sb * ca + sc * sa],
        [sc * cb, sc * sb * sa + cc * ca, sc * sb * ca - cc * sa],
        [-sb, cb * sa, cb * ca],
    ]
    shift = [cameras[:, 3], cameras[:, 4], cameras[:, 5]]
    anchor = [-sum(turn[i][e] * shift[i] for i in range(3)) for e in range(3)]
    return jnp.stack(turn[0] + turn[1] + turn[2] + shift + anchor + [shift[0]], axis=1)


def harmonics(x, y, z):
    xx, yy, zz = x * x, y * y, z * z
    return [
        SH_ZERO * jnp.ones_like(x),
        -SH_ONE * y,
        SH_ONE * z,
        -SH_ONE * x,
        SH_TWO[0] * x * y,
        SH_TWO[1] * y * z,
        SH_TWO[2] * (2.0 * zz - xx - yy),
        SH_TWO[3] * x * z,
        SH_TWO[4] * (xx - yy),
        SH_THREE[0] * y * (3.0 * xx - yy),
        SH_THREE[1] * x * y * z,
        SH_THREE[2] * y * (4.0 * zz - xx - yy),
        SH_THREE[3] * z * (2.0 * zz - 3.0 * xx - 3.0 * yy),
        SH_THREE[4] * x * (4.0 * zz - xx - yy),
        SH_THREE[5] * z * (xx - yy),
        SH_THREE[6] * x * (xx - 3.0 * yy),
    ]


def shape_of(scales, rots):
    inv = 1.0 / jnp.sqrt(sum(q * q for q in rots))
    s, x, y, z = [q * inv for q in rots]
    turn = [
        [1.0 - 2.0 * (y * y + z * z), 2.0 * (x * y - s * z), 2.0 * (x * z + s * y)],
        [2.0 * (x * y + s * z), 1.0 - 2.0 * (x * x + z * z), 2.0 * (y * z - s * x)],
        [2.0 * (x * z - s * y), 2.0 * (y * z + s * x), 1.0 - 2.0 * (x * x + y * y)],
    ]
    spread = [jnp.exp(v) for v in scales]
    m = [[turn[i][e] * spread[e] for e in range(3)] for i in range(3)]
    pairs = ((0, 0), (0, 1), (0, 2), (1, 1), (1, 2), (2, 2))
    return [sum(m[i][e] * m[k][e] for e in range(3)) for i, k in pairs]


def geometry(centers, sigma, cam, width_px, height_px):
    pts = [
        sum(cam[3 * i + e] * centers[e] for e in range(3)) + cam[9 + i] for i in range(3)
    ]
    inv = 1.0 / pts[2]
    diag = FOCAL * inv
    ux, uy = pts[0] * inv, pts[1] * inv
    row_x = [diag * (cam[e] - ux * cam[6 + e]) for e in range(3)]
    row_y = [diag * (cam[3 + e] - uy * cam[6 + e]) for e in range(3)]
    sxx, sxy, sxz, syy, syz, szz = sigma
    full = [[sxx, sxy, sxz], [sxy, syy, syz], [sxz, syz, szz]]
    half_x = [sum(full[i][e] * row_x[e] for e in range(3)) for i in range(3)]
    half_y = [sum(full[i][e] * row_y[e] for e in range(3)) for i in range(3)]
    cov_xx = sum(row_x[i] * half_x[i] for i in range(3)) + BLUR
    cov_xy = sum(row_y[i] * half_x[i] for i in range(3))
    cov_yy = sum(row_y[i] * half_y[i] for i in range(3)) + BLUR
    det = 1.0 / (cov_xx * cov_yy - cov_xy * cov_xy)
    return [
        FOCAL * ux + 0.5 * width_px,
        FOCAL * uy + 0.5 * height_px,
        cov_yy * det,
        -cov_xy * det,
        cov_xx * det,
    ]


def direction_basis(centers, cam):
    off = [centers[e] - cam[12 + e] for e in range(3)]
    inv = 1.0 / jnp.sqrt(sum(v * v for v in off))
    return harmonics(*[v * inv for v in off])


def small_row(small_ref, index, chunk):
    return small_ref[index, pl.ds(pl.multiple_of(chunk * 8, 8), 8), :]


def harm_slice(row, chunk):
    return pl.ds(((row // 8) * BLOCKS + chunk * 8) * 8 + row % 8, 8, stride=8)


def gather_blocks(tbl, index_hi, index_lo):
    acc = [jnp.zeros((8, LANES), F32) for _ in range(5)]
    for b in range(BLOCKS):
        hit = index_hi == b
        for i in range(5):
            got = jnp.take_along_axis(
                tbl[b * TBL + 8 * i : b * TBL + 8 * i + 8, :],
                index_lo,
                axis=1,
                mode="promise_in_bounds",
            )
            acc[i] = jnp.where(hit, got, acc[i])
    return acc


def slot_place(o):
    return (o // 16) * 8 + o % 8, (o // 8) % 2


def splat_out(width_px, height_px, cam_ref, small_ref, harm_ref, ids_ref, out_ref, tbl):
    def chunk_step(chunk, carry):
        centers = [small_row(small_ref, i, chunk) for i in range(3)]
        scales = [small_row(small_ref, 3 + i, chunk) for i in range(3)]
        rots = [small_row(small_ref, 6 + i, chunk) for i in range(4)]
        opacity = jax.nn.sigmoid(small_row(small_ref, 10, chunk))
        sigma = shape_of(scales, rots)
        base = chunk * (8 * TBL)
        for view in range(VIEWS):
            cam = [cam_ref[view, i] for i in range(15)]
            record = geometry(centers, sigma, cam, width_px, height_px) + [opacity]
            basis = direction_basis(centers, cam)
            for colour in range(3):
                total = sum(
                    harm_ref[harm_slice(colour * 16 + i, chunk), :] * basis[i]
                    for i in range(16)
                )
                record.append(jnp.maximum(total + 0.5, 0.0))
            for i in range(8):
                tbl[pl.ds(base + view * 8 + i, 8, stride=TBL), :] = record[i]
            tbl[pl.ds(base + 32 + view, 8, stride=TBL), :] = record[8]
        return carry

    lax.fori_loop(0, BLOCKS // 8, chunk_step, 0)

    def order_step(o, carry):
        index = jnp.broadcast_to(ids_ref[pl.ds(o, 1), :], (8, LANES))
        acc = gather_blocks(tbl, index >> 7, index & 127)
        owner, half = slot_place(o)
        for view in range(VIEWS):
            row = (view * 32 + owner) * MSG + half
            out_ref[pl.ds(row, 8, stride=2), :] = acc[view]
            out_ref[pl.ds(row + 16, 1), :] = acc[4][view : view + 1, :]
        return carry

    lax.fori_loop(0, BLOCKS, order_step, 0)


def top_f32(x):
    return x.astype(BF16).astype(F32)


def split(x):
    top = x.astype(BF16)
    return top, x - top.astype(F32)


def product(x, y):
    return jnp.dot(x, y, preferred_element_type=F32)


def summed(x, pattern):
    top, rest = split(x)
    return product(jnp.concatenate([top, rest.astype(BF16)], axis=1), pattern)


def tiles(
    perm_ref, recv_ref, list_ref, target_ref, out_ref, image_ref, loss_ref,
    tab, wide, target_t, image_t, rec, alpha, weight, ends, shades, prefix, res, behind,
    moments, grad, inverse, sums_ref,
):
    lane = lax.broadcasted_iota(I32, (8, LANES), 1)
    sub = lax.broadcasted_iota(I32, (8, LANES), 0)
    sub_f = sub.astype(F32)
    tall_lane = lax.broadcasted_iota(I32, (256, LANES), 1)
    from_lane = lax.broadcasted_iota(I32, (256, LANES), 0) % 128
    sums_ref[0] = (from_lane < tall_lane).astype(F32).astype(BF16)
    sums_ref[1] = jnp.ones((256, LANES), BF16)
    sums_ref[2] = (from_lane > tall_lane).astype(F32).astype(BF16)

    for half in range(2):
        for k in range(FIELDS):
            tab[k, half * 128 : half * 128 + 128, :] = recv_ref[
                pl.ds(k * 2 + half, 128, stride=MSG), :
            ].T
    wide[...] = jnp.zeros_like(wide)
    wide[0:48, :] = target_ref[...]
    for i in range(2):
        target_t[i * 128 : i * 128 + 128, :] = wide[:, i * 128 : i * 128 + 128].T
    image_t[...] = jnp.zeros_like(image_t)

    def take(x, index):
        return jnp.take_along_axis(x, index, axis=1, mode="promise_in_bounds")

    def tile_step(r, loss):
        place = perm_ref[r]
        ox = (16 * (place % TW)).astype(F32)
        oy = (16 * (place // TW)).astype(F32)
        row0 = (r // 8) * 128 + r % 8
        list_lo = list_ref[pl.ds(row0, 8, stride=8), :].astype(F32)
        list_hi = list_ref[pl.ds(row0 + 64, 8, stride=8), :].astype(F32)
        count = jnp.sum(
            (list_lo >= 0.0).astype(F32) + (list_hi >= 0.0).astype(F32)
        ).astype(I32)
        steps = (count + 127) // 128
        inverse[...] = jnp.zeros_like(inverse)
        tile_rows = pl.multiple_of(r * 16, 8)

        def load_step(j, carry):
            k = lane * steps + j
            block, low = k >> 7, k & 127
            entry = jnp.sum(
                jnp.where(block == sub, take(list_lo, low), 0.0)
                + jnp.where(block == sub + 8, take(list_hi, low), 0.0),
                axis=0,
                keepdims=True,
            ).astype(I32)
            entry = jnp.broadcast_to(entry, (8, LANES))
            source, slot = (entry >> 8) & 127, entry & 15
            hit0, hit1 = slot == sub, slot == sub + 8
            fields = []
            for f in range(FIELDS):
                got0 = take(tab[f, pl.ds(tile_rows, 8), :], source)
                got1 = take(tab[f, pl.ds(tile_rows + 8, 8), :], source)
                fields.append(
                    jnp.sum(
                        jnp.where(hit0, got0, jnp.where(hit1, got1, 0.0)),
                        axis=0,
                        keepdims=True,
                    )
                )
            listed = entry[0:1] >= 0
            mx, my = fields[0] - ox, fields[1] - oy
            opacity = jnp.where(listed, fields[5], 1.0)
            level = jnp.where(listed, jnp.log2(opacity), -1e30)
            for i, value in enumerate(
                [mx, my] + fields[2:5] + [opacity] + fields[6:9]
            ):
                rec[j, pl.ds(i, 1), :] = value
            qxx = (-0.5 * LOG2E) * fields[2]
            qxy = -LOG2E * fields[3]
            qyy = (-0.5 * LOG2E) * fields[4]
            parts = []
            for h in range(2):
                dx = (sub_f + 8.0 * h) - mx
                parts.append((qxy * dx, qxx * dx * dx + level))
            for y in range(16):
                dy = jnp.broadcast_to(float(y) - my, (8, LANES))
                turn = qyy * dy
                for h in range(2):
                    slope, level_h = parts[h]
                    alpha[j, y * 2 + h] = jnp.exp2((slope + turn) * dy + level_h)
            rows = lax.broadcasted_iota(I32, (128, LANES), 0)
            listed_b = entry >= 0
            one_hot = (rows == entry[0:1] >> 8).astype(F32)
            step_no = (j + 1).astype(F32)
            left = [
                jnp.where(hit0 & listed_b, step_no, 0.0),
                jnp.where(hit1 & listed_b, step_no, 0.0),
                jnp.where(hit0 & listed_b, lane.astype(F32), 0.0),
                jnp.where(hit1 & listed_b, lane.astype(F32), 0.0),
            ]
            inverse[...] += lax.dot_general(
                jnp.concatenate(left, axis=0).astype(BF16),
                one_hot.astype(BF16),
                (((1,), (1,)), ((), ())),
                preferred_element_type=F32,
            )
            return carry

        lax.fori_loop(0, steps, load_step, 0)

        for g in range(4):

            def front_step(j, carry):
                keep, col = list(carry[:8]), list(carry[8:])
                shade = [
                    jnp.broadcast_to(rec[j, pl.ds(6 + c, 1), :], (8, LANES)) for c in range(3)
                ]
                for i in range(8):
                    w = alpha[j, g * 8 + i] * keep[i]
                    weight[j, g * 8 + i] = w
                    keep[i] = keep[i] - w
                    for c in range(3):
                        col[i * 3 + c] = col[i * 3 + c] + shade[c] * w
                return tuple(keep + col)

            start = [jnp.ones((8, LANES), F32)] * 8 + [jnp.zeros((8, LANES), F32)] * 24
            done = lax.fori_loop(0, steps, front_step, tuple(start))
            for i in range(8):
                ends[g * 8 + i] = done[i]
                for c in range(3):
                    shades[c, g * 8 + i] = done[8 + i * 3 + c]

        def all_pixels(x):
            return x.reshape(256, LANES)

        local_end = all_pixels(ends[...])
        level_end = jnp.log2(local_end)
        top, rest_bits = split(level_end)
        low = (rest_bits - top_f32(rest_bits)).astype(BF16)
        front = jnp.exp2(
            product(jnp.concatenate([top, rest_bits.astype(BF16)], axis=1), sums_ref[0])
            + product(low, sums_ref[0, 0:128, :])
        )
        prefix[...] = front.reshape(32, 8, LANES)
        target = target_t[...]
        image = image_t[...]
        behind_all = jnp.zeros((256, LANES), F32)
        square = jnp.zeros((256, LANES), F32)
        for c in range(3):
            part = front * all_pixels(shades[c])
            mine = tall_lane == c * 16 + r
            diff = summed(part - jnp.where(mine, target, 0.0), sums_ref[1])
            res[c] = diff.reshape(32, 8, LANES)
            image = jnp.where(mine, diff + target, image)
            behind_all = behind_all + diff * part
            square = square + diff * diff
        image_t[...] = image
        behind[...] = (summed(behind_all, sums_ref[2]) / (front * local_end)).reshape(
            32, 8, LANES
        )
        loss = loss + jnp.sum(square.reshape(32, 8, LANES), axis=0)

        for g in range(4):

            def back_step(back_j, carry):
                back = list(carry)
                j = steps - 1 - back_j
                shade = [
                    jnp.broadcast_to(rec[j, pl.ds(6 + c, 1), :], (8, LANES)) for c in range(3)
                ]
                if g == 0:
                    sums = [jnp.zeros((8, LANES), F32)] * 9
                else:
                    sums = [moments[j, i] for i in range(9)]
                for i in range(8):
                    idx = g * 8 + i
                    h = i % 2
                    a = alpha[j, idx]
                    w = weight[j, idx] * prefix[idx]
                    diff = [res[c, idx] for c in range(3)]
                    u = shade[0] * diff[0] + shade[1] * diff[1] + shade[2] * diff[2] - back[i]
                    back[i] = back[i] + a * u
                    v = w * u
                    for c in range(3):
                        sums[6 + c] = sums[6 + c] + diff[c] * w
                    sums[3 * h] = sums[3 * h] + v
                    sums[3 * h + 1] = sums[3 * h + 1] + sums[3 * h]
                    sums[3 * h + 2] = sums[3 * h + 2] + sums[3 * h + 1]
                for i in range(9):
                    moments[j, i] = sums[i]
                return tuple(back)

            lax.fori_loop(0, steps, back_step, tuple(behind[g * 8 + i] for i in range(8)))

        def finish_step(j, carry):
            def total(x):
                return jnp.sum(x, axis=0, keepdims=True)

            s = [moments[j, i] for i in range(9)]
            x0, x1 = sub_f, sub_f + 8.0
            y1 = [16.0 * s[3 * h] - s[3 * h + 1] for h in range(2)]
            y2 = [256.0 * s[3 * h] - 33.0 * s[3 * h + 1] + 2.0 * s[3 * h + 2] for h in range(2)]
            m0 = total(s[0] + s[3])
            m_x = total(x0 * s[0] + x1 * s[3])
            m_xx = total(x0 * x0 * s[0] + x1 * x1 * s[3])
            m_y = total(y1[0] + y1[1])
            m_xy = total(x0 * y1[0] + x1 * y1[1])
            m_yy = total(y2[0] + y2[1])
            mx, my, xx, xy, yy, opacity = [rec[j, pl.ds(i, 1), :] for i in range(6)]
            g_x = m_x - mx * m0
            g_y = m_y - my * m0
            g_xx = m_xx - 2.0 * mx * m_x + mx * mx * m0
            g_xy = m_xy - mx * m_y - my * m_x + mx * my * m0
            g_yy = m_yy - 2.0 * my * m_y + my * my * m0
            out = [
                xx * g_x + xy * g_y,
                yy * g_y + xy * g_x,
                -0.5 * g_xx,
                -g_xy,
                -0.5 * g_yy,
                m0 / opacity,
            ] + [total(s[6 + c]) for c in range(3)]
            for i in range(FIELDS):
                grad[j, pl.ds(i, 1), :] = out[i]
            return carry

        lax.fori_loop(0, steps, finish_step, 0)

        step0 = inverse[0:8, :].astype(I32)
        step1 = inverse[8:16, :].astype(I32)
        lane0 = inverse[16:24, :].astype(I32)
        lane1 = inverse[24:32, :].astype(I32)

        def unlist_step(j, carry):
            acc = list(carry)
            hit0, hit1 = step0 == j + 1, step1 == j + 1
            for f in range(FIELDS):
                row = jnp.broadcast_to(grad[j, pl.ds(f, 1), :], (8, LANES))
                acc[2 * f] = jnp.where(hit0, take(row, lane0), acc[2 * f])
                acc[2 * f + 1] = jnp.where(hit1, take(row, lane1), acc[2 * f + 1])
            return tuple(acc)

        acc = lax.fori_loop(0, steps, unlist_step, (jnp.zeros((8, LANES), F32),) * 18)
        for f in range(FIELDS):
            tab[f, pl.ds(tile_rows, 8), :] = acc[2 * f]
            tab[f, pl.ds(tile_rows + 8, 8), :] = acc[2 * f + 1]
        return loss

    loss = lax.fori_loop(0, 16, tile_step, jnp.zeros((8, LANES), F32))
    loss_ref[...] = loss
    for half in range(2):
        for k in range(FIELDS):
            out_ref[pl.ds(k * 2 + half, 128, stride=MSG), :] = tab[
                k, half * 128 : half * 128 + 128, :
            ].T
    for i in range(2):
        wide[:, i * 128 : i * 128 + 128] = image_t[i * 128 : i * 128 + 128, :].T
    image_ref[...] = wide[0:48, :]


def splat_back(
    width_px, height_px, cam_ref, small_ref, harm_ref, ids_ref, ret_ref,
    gsmall_ref, gharm_ref, tbl, nat, inverse,
):
    lane = lax.broadcasted_iota(I32, (1, LANES), 1)
    rows64 = lax.broadcasted_iota(I32, (BLOCKS, LANES), 0)
    rows128 = lax.broadcasted_iota(I32, (LANES, LANES), 0)
    inverse[...] = jnp.zeros_like(inverse)

    def invert_step(o, carry):
        index = ids_ref[pl.ds(o, 1), :]
        hit = rows64 == index >> 7
        one_hot = (rows128 == index & 127).astype(F32).astype(BF16)
        left = jnp.concatenate(
            [
                jnp.where(hit, (o + 1).astype(F32), 0.0),
                jnp.where(hit, lane.astype(F32), 0.0),
            ],
            axis=0,
        )
        inverse[...] += lax.dot_general(
            left.astype(BF16),
            one_hot,
            (((1,), (1,)), ((), ())),
            preferred_element_type=F32,
        )
        owner, half = slot_place(o)
        base = o * TBL
        for view in range(VIEWS):
            row = (view * 32 + owner) * MSG + half
            tbl[pl.ds(base + view * 8, 8), :] = ret_ref[pl.ds(row, 8, stride=2), :]
            tbl[pl.ds(base + 32 + view, 1), :] = ret_ref[pl.ds(row + 16, 1), :]
        return carry

    lax.fori_loop(0, BLOCKS, invert_step, 0)

    def order_step(n, carry):
        block = jnp.broadcast_to(inverse[pl.ds(n, 1), :].astype(I32) - 1, (8, LANES))
        low = jnp.broadcast_to(inverse[pl.ds(BLOCKS + n, 1), :].astype(I32), (8, LANES))
        acc = gather_blocks(tbl, block, low)
        for i in range(5):
            nat[pl.ds(8 * i * BLOCKS + n, 8, stride=BLOCKS), :] = acc[i]
        return carry

    lax.fori_loop(0, BLOCKS, order_step, 0)

    def chunk_step(chunk, carry):
        centers = [small_row(small_ref, i, chunk) for i in range(3)]
        scales = [small_row(small_ref, 3 + i, chunk) for i in range(3)]
        rots = [small_row(small_ref, 6 + i, chunk) for i in range(4)]
        opacity = jax.nn.sigmoid(small_row(small_ref, 10, chunk))

        def given(view, i):
            row = view * 8 + i if i < 8 else 32 + view
            return nat[pl.ds(pl.multiple_of(row * BLOCKS + chunk * 8, 8), 8), :]

        sigma, shape_pull = jax.vjp(shape_of, scales, rots)
        d_centers = [jnp.zeros((8, LANES), F32)] * 3
        d_sigma = [jnp.zeros((8, LANES), F32)] * 6
        d_opacity = jnp.zeros((8, LANES), F32)
        for view in range(VIEWS):
            cam = [cam_ref[view, i] for i in range(15)]
            _, geo_pull = jax.vjp(
                lambda c, s: geometry(c, s, cam, width_px, height_px), centers, sigma
            )
            d_c, d_s = geo_pull([given(view, i) for i in range(5)])
            basis, dir_pull = jax.vjp(lambda c: direction_basis(c, cam), centers)
            d_opacity = d_opacity + given(view, 5)
            d_basis = [jnp.zeros((8, LANES), F32)] * 16
            for colour in range(3):
                rows = [harm_slice(colour * 16 + i, chunk) for i in range(16)]
                coeffs = [harm_ref[row, :] for row in rows]
                total = sum(coeffs[i] * basis[i] for i in range(16)) + 0.5
                slope = jnp.where(total > 0.0, 1.0, jnp.where(total == 0.0, 0.5, 0.0))
                d_total = given(view, 6 + colour) * slope
                for i in range(16):
                    d_basis[i] = d_basis[i] + d_total * coeffs[i]
                    term = d_total * basis[i]
                    if view == 0:
                        gharm_ref[rows[i], :] = term
                    else:
                        gharm_ref[rows[i], :] = gharm_ref[rows[i], :] + term
            (d_dir,) = dir_pull(d_basis)
            d_centers = [d_centers[e] + d_c[e] + d_dir[e] for e in range(3)]
            d_sigma = [d_sigma[e] + d_s[e] for e in range(6)]
        d_scales, d_rots = shape_pull(d_sigma)
        values = (
            list(d_centers)
            + list(d_scales)
            + list(d_rots)
            + [d_opacity * opacity * (1.0 - opacity)]
        )
        for i in range(11):
            gsmall_ref[i, pl.ds(pl.multiple_of(chunk * 8, 8), 8), :] = values[i]
        return carry

    lax.fori_loop(0, BLOCKS // 8, chunk_step, 0)


def tile_order(x):
    rows, width = x.shape
    split = x.reshape(rows // 8, 8, width // LANES, LANES)
    return split.transpose(0, 2, 1, 3).reshape(rows * width // LANES, LANES)


def from_tile_order(x, rows):
    width = x.shape[0] * LANES // rows
    split = x.reshape(rows // 8, width // LANES, 8, LANES)
    return split.transpose(0, 2, 1, 3).reshape(rows, width)


def params(mib):
    return pltpu.CompilerParams(vmem_limit_bytes=mib * 1024 * 1024)


def shape(*dims):
    return jax.ShapeDtypeStruct(dims, F32)


VM = functools.partial(pl.BlockSpec, memory_space=pltpu.VMEM)
SM = functools.partial(pl.BlockSpec, memory_space=pltpu.SMEM)


def exchange(message):
    blocks = message.reshape(128, MSG, LANES)
    return lax.all_to_all(
        blocks, ("view", "pix"), split_axis=0, concat_axis=0, tiled=True
    ).reshape(128 * MSG, LANES)


def local(
    centers, log_scales, rotations, logits, harmonic_coeffs,
    cameras, send_ids, tile_lists, tile_perm, targets,
):
    width_px = 16 * TW
    height_px = 16 * (512 // TW)
    cam = camera_numbers(cameras)
    small = jnp.concatenate(
        [centers, log_scales, rotations, logits[None]], axis=0
    ).reshape(11, BLOCKS, LANES)
    harm = tile_order(harmonic_coeffs)
    ids = tile_order(send_ids[0])
    sending = pl.pallas_call(
        functools.partial(splat_out, width_px, height_px),
        out_shape=shape(128 * MSG, LANES),
        in_specs=[SM(), VM(), VM(), VM()],
        out_specs=VM(),
        scratch_shapes=[pltpu.VMEM((BLOCKS * TBL, LANES), F32)],
        compiler_params=params(32),
        name="splat_out",
    )(cam, small, harm, ids)
    received = exchange(sending)
    vreg = (8, LANES)
    returning, image, loss = pl.pallas_call(
        tiles,
        out_shape=(shape(128 * MSG, LANES), shape(48, 256), shape(8, LANES)),
        in_specs=[SM(), VM(), VM(), VM()],
        out_specs=(VM(), VM(), VM()),
        scratch_shapes=[
            pltpu.VMEM((FIELDS, 256, LANES), F32),
            pltpu.VMEM((LANES, 256), F32),
            pltpu.VMEM((256, LANES), F32),
            pltpu.VMEM((256, LANES), F32),
            pltpu.VMEM((16, 16, LANES), F32),
            pltpu.VMEM((16, 32) + vreg, F32),
            pltpu.VMEM((16, 32) + vreg, F32),
            pltpu.VMEM((32,) + vreg, F32),
            pltpu.VMEM((3, 32) + vreg, F32),
            pltpu.VMEM((32,) + vreg, F32),
            pltpu.VMEM((3, 32) + vreg, F32),
            pltpu.VMEM((32,) + vreg, F32),
            pltpu.VMEM((16, 9) + vreg, F32),
            pltpu.VMEM((16, 16, LANES), F32),
            pltpu.VMEM((32, LANES), F32),
            pltpu.VMEM((3, 256, LANES), BF16),
        ],
        compiler_params=params(48),
        name="tiles",
    )(
        tile_perm,
        received,
        tile_order(tile_lists),
        targets[0].transpose(1, 0, 2).reshape(48, 256),
    )
    returned = exchange(returning)
    total_loss = lax.psum(0.5 * jnp.sum(loss[:, 0]), ("view", "pix"))
    gsmall, gharm = pl.pallas_call(
        functools.partial(splat_back, width_px, height_px),
        out_shape=(shape(11, BLOCKS, LANES), shape(48 * BLOCKS, LANES)),
        in_specs=[SM(), VM(), VM(), VM(), VM()],
        out_specs=(VM(), VM()),
        scratch_shapes=[
            pltpu.VMEM((BLOCKS * TBL, LANES), F32),
            pltpu.VMEM((BLOCKS * TBL, LANES), F32),
            pltpu.VMEM((2 * BLOCKS, LANES), F32),
        ],
        compiler_params=params(32),
        name="splat_back",
    )(cam, small, harm, ids, returned)
    flat = gsmall.reshape(11, BLOCKS * LANES)
    rendered = image.reshape(3, 16, 256).transpose(1, 0, 2)[None]
    return (
        rendered,
        total_loss,
        flat[0:3],
        flat[3:6],
        flat[6:10],
        flat[10],
        from_tile_order(gharm, 48),
    )


def solution(mesh):
    both = ("view", "pix")
    return jax.shard_map(
        local,
        mesh=mesh,
        in_specs=(
            P(None, both),
            P(None, both),
            P(None, both),
            P(both),
            P(None, both),
            P(),
            P(both, None, None),
            P("pix", None),
            P("pix"),
            P("view", "pix", None, None),
        ),
        out_specs=(
            P("view", "pix", None, None),
            P(),
            P(None, both),
            P(None, both),
            P(None, both),
            P(both),
            P(None, both),
        ),
        check_vma=False,
    )
```

time: 2470 us -> 293 us (0.12); the launches traced: 2440 us -> 289 us
  other arithmetic: 1030 us -> 3.13 us
  local copies, waits for them, and re-layouts: 746 us -> 7.65 us
  matrix products: 381 us -> 0 us
  Pallas kernels: 0 us -> 139 us
  loops' own time: 104 us -> 0 us
  between operations: 46.6 us -> 1.38 us
  waiting for transfers between devices: 27.7 us -> 0.01 us
  blocking collectives: 80.5 us -> 108 us
    scatter-add x21 -> x0, other arithmetic: 426 us -> none  [the longest x5 237 us: outgoing(): picked = [jnp.take(param, safe_ids, axis=-1) for param in params]]
    dot_general x384 -> x0, matrix products: 381 us -> none  [the longest x128 170 us: second_pass(): shade = jnp.dot(residual.T, piece[6:9], precision=full_precision)]
    gather x25 -> x0, local copies, waits for them, and re-layouts: 312 us -> none  [the longest x9 225 us: outgoing(): picked = [jnp.take(param, safe_ids, axis=-1) for param in params]]
    mul x207 -> x0, other arithmetic: 178 us -> none  [the longest x128 126 us: alpha_of(): return record[5][None, :] * jnp.exp(exponent)]
    another operation x791 -> x0, other arithmetic: 159 us -> none
    pallas_call x0 -> x3, Pallas kernels: none -> 139 us  [the longest x1 65.1 us: local(): pl.pallas_call(tiles, out_shape=(shape(128 * MSG, LANES), shape(48, 256),...]
    reduce_sum x157 -> x1, other arithmetic: 122 us -> 0.6 us  [local(): total_loss = lax.psum(0.5 * jnp.sum(loss[:, 0]), ('view', 'pix'))]
    slice x514 -> x1, local copies, waits for them, and re-layouts: 106 us -> 0.89 us  [camera_numbers(): shift = [cameras[:, 3], cameras[:, 4], cameras[:, 5]]]
where the time goes in v1:
time: 293 us; the launch traced here: 289 us
  Pallas kernels  139 us (47%)
  blocking collectives  108 us (37%)
  starting transfers between devices  30.5 us (10%)
  local copies, waits for them, and re-layouts  7.65 us (3%)
  other arithmetic  3.13 us (1%)
    psum x1, blocking collectives, local(): total_loss = lax.psum(0.5 * jnp.sum(loss[:, 0]), ('view', 'pix'))  74.3 us
    pallas_call x1, Pallas kernels, local(): pl.pallas_call(tiles, out_shape=(shape(128 * MSG, LANES), shape(48, 256),...  65.1 us
    pallas_call x1, Pallas kernels, local(): pl.pallas_call(functools.partial(splat_back, width_px, height_px), out_sh...  45.4 us
    all_to_all x1, blocking collectives, exchange(): lax.all_to_all(blocks, ('view', 'pix'), split_axis=0, concat_axis=0, tile...  33.4 us
    all_to_all x1, starting transfers between devices, exchange(): lax.all_to_all(blocks, ('view', 'pix'), split_axis=0, concat_axis=0, tile...  30.5 us
    pallas_call x1, Pallas kernels, local(): pl.pallas_call(functools.partial(splat_out, width_px, height_px), out_sha...  28.6 us
  transfers between devices with their start and end apart: 1, of which 0 were waited for; matrix products, arithmetic and copies ran while one was open for 0% of the time, Pallas kernels for 0%

profile of v1, /device:TPU:25, one launch (start us, length us, event | category | flops | bytes accessed | tf_op | source)
XLA Modules:
  0.0 289.4 jit_solution(17817330985369214495)
XLA Ops:
  0.6 0.0 copy-start
  0.6 0.9 fusion
  1.5 0.9 add_negate_fusion.1
  2.4 0.9 add_negate_fusion
  3.3 0.9 copy.32
  4.2 1.0 copy_bitcast_fusion.4
  5.2 0.8 pad_maximum_fusion.small_ref
  6.0 0.1 stack.2.cam_ref
  6.1 0.0 copy-done
  6.1 0.0 copy-start.2
  6.1 0.7 copy-done.2
  6.8 28.6 %splat_out.1 = f32[3072,128]{1,0:T(8,128)S(1)} custom-call(f32[4,16]{1,0:T(4,128)S(1)} %stack.2.cam_ref, f32[11,64,128]{2,1,0:T(8,128)S(1)} %pad_maximum_fusion.small_ref, f32[3072,128]{1,0:T(8,128)S(1)} %bitcast.62, s32[64,128]{1,0:T(8,128)S(1)} %bitcast.68), custom_call_target="tpu_custom_call" | custom-call | tf_op jit(solution)/shard_map/splat_out/pallas_call | solution.py:606
  35.4 0.0 copy-start.4
  35.4 0.0 copy-start.5
  35.4 0.0 copy-start.6
  35.5 33.4 %all_to_all.10 = f32[128,24,128]{2,1,0:T(8,128)S(1)} all-to-all(f32[128,24,128]{2,1,0:T(8,128)S(1)} %bitcast.66), channel_id=1, replica_groups=mesh['view'=4,'pix'=32] {'view','pix'}, dimensions={0} | all-to-all | bytes 3145728 | tf_op jit(solution)/shard_map/all_to_all | solution.py:589
  68.9 0.0 copy-done.4
  68.9 0.0 copy-done.5
  68.9 0.0 copy-done.6
  68.9 65.1 %tiles.1 = (f32[3072,128]{1,0:T(8,128)S(1)}, f32[48,256]{1,0:T(8,128)}, f32[8,128]{1,0:T(8,128)S(1)}) custom-call(s32[16]{0:T(128)S(1)} %copy-done.6, f32[3072,128]{1,0:T(8,128)S(1)} %bitcast.65, s32[256,128]{1,0:T(8,128)S(1)} %bitcast.70, f32[48,256]{1,0:T(8,128)S(1)} %bitcast.71), custom_call_target="tpu_custom_call" | custom-call | tf_op jit(solution)/shard_map/tiles/pallas_call | solution.py:617
  134.0 0.0 copy-start.1
  134.0 1.1 copy-done.1
  135.1 0.0 copy-start.3
  135.1 30.5 %all-to-all-start.1 = ((f32[128,24,128]{2,1,0:T(8,128)}), f32[128,24,128]{2,1,0:T(8,128)S(1)}, u32[]{:S(2)}, u32[]{:S(2)}) async-start(f32[128,24,128]{2,1,0:T(8,128)} %bitcast.67), calls=%async_computation.1 | async-start | bytes 3145728 | tf_op jit(solution)/shard_map/all_to_all | solution.py:589
  165.6 0.6 slice_reduce_fusion
  166.8 74.3 %psum.7 = f32[]{:T(128)} all-reduce(f32[]{:T(128)S(6)} %mul_shard_map.3), channel_id=1, replica_groups=mesh['view'=4,'pix'=32] {'view','pix'}, use_global_device_ids=true, to_apply=%region_1.0 | all-reduce | flops 1 | bytes 8 | tf_op jit(solution)/shard_map/psum | solution.py:649
  241.1 0.0 all-to-all-done.1
  241.1 0.0 copy-done.3
  241.1 45.4 %splat_back.1 = (f32[11,64,128]{2,1,0:T(8,128)S(1)}, f32[3072,128]{1,0:T(8,128)}) custom-call(f32[4,16]{1,0:T(4,128)S(1)} %stack.2.cam_ref, f32[11,64,128]{2,1,0:T(8,128)S(1)} %pad_maximum_fusion.small_ref, f32[3072,128]{1,0:T(8,128)S(1)} %bitcast.63, s32[64,128]{1,0:T(8,128)S(1)} %bitcast.69, f32[3072,128]{1,0:T(8,128)S(1)} %bitcast.64), custom_call_target="tpu_custom_call" | custom-call | tf_op jit(solution)/shard_map/splat_back/pallas_call | solution.py:650
  286.5 0.6 slice_bitcast_fusion.3
  287.2 0.7 copy.29
  287.9 0.7 copy.30
  288.6 0.7 copy.31
  (2 shorter events, 0.0 us)
Async XLA Ops:
  0.6 5.5 %copy-start = (f32[48,8192]{1,0:T(8,128)S(1)}, f32[48,8192]{1,0:T(8,128)}, u32[]{:S(2)}) copy-start(f32[48,8192]{1,0:T(8,128)} %param.14) | copy-start | bytes 4718596
  6.1 0.8 copy-start.2
  35.4 33.5 %copy-start.4 = (s32[16,2048]{1,0:T(8,128)S(1)}, s32[16,2048]{1,0:T(8,128)}, u32[]{:S(2)}) copy-start(s32[16,2048]{1,0:T(8,128)} %param.17) | copy-start | bytes 393220
  35.4 33.5 %copy-start.5 = (f32[1,16,3,256]{3,1,2,0:T(8,128)S(1)}, f32[1,16,3,256]{3,1,2,0:T(8,128)}, u32[]{:S(2)}) copy-start(f32[1,16,3,256]{3,1,2,0:T(8,128)} %param.19) | copy-start | bytes 147460
  35.4 33.4 %copy-start.6 = (s32[16]{0:T(128)S(1)}, s32[16]{0:T(128)}, u32[]{:S(2)}) copy-start(s32[16]{0:T(128)} %perm_ref.1) | copy-start | bytes 196
  134.0 1.1 copy-start.1
  135.1 106.0 %copy-start.3 = (s32[1,32,256]{2,1,0:T(8,128)S(1)}, s32[1,32,256]{2,1,0:T(8,128)}, u32[]{:S(2)}) copy-start(s32[1,32,256]{2,1,0:T(8,128)} %param.16) | copy-start | bytes 98308
  135.1 106.0 %all-to-all-start.1 = ((f32[128,24,128]{2,1,0:T(8,128)}), f32[128,24,128]{2,1,0:T(8,128)S(1)}, u32[]{:S(2)}, u32[]{:S(2)}) async-start(f32[128,24,128]{2,1,0:T(8,128)} %bitcast.67), calls=%async_computation.1 | async-start | bytes 3145728 | tf_op jit(solution)/shard_map/all_to_all | solution.py:589

commit v2 on v1

--- a/solution.py
+++ b/solution.py
@@ -33,6 +33,7 @@
 VIEWS = 4
 FIELDS = 9
 MSG = 24
+LOSS_ROW = 18
 TBL = 40
 BLOCKS = 64
 F32 = jnp.float32
@@ -130,26 +131,11 @@
     return pl.ds(((row // 8) * BLOCKS + chunk * 8) * 8 + row % 8, 8, stride=8)
 
 
-def gather_blocks(tbl, index_hi, index_lo):
-    acc = [jnp.zeros((8, LANES), F32) for _ in range(5)]
-    for b in range(BLOCKS):
-        hit = index_hi == b
-        for i in range(5):
-            got = jnp.take_along_axis(
-                tbl[b * TBL + 8 * i : b * TBL + 8 * i + 8, :],
-                index_lo,
-                axis=1,
-                mode="promise_in_bounds",
-            )
-            acc[i] = jnp.where(hit, got, acc[i])
-    return acc
-
-
 def slot_place(o):
     return (o // 16) * 8 + o % 8, (o // 8) % 2
 
 
-def splat_out(width_px, height_px, cam_ref, small_ref, harm_ref, ids_ref, out_ref, tbl):
+def splat_out(width_px, height_px, cam_ref, small_ref, harm_ref, ids_ref, out_ref, tbl, by_row, stage):
     def chunk_step(chunk, carry):
         centers = [small_row(small_ref, i, chunk) for i in range(3)]
         scales = [small_row(small_ref, 3 + i, chunk) for i in range(3)]
@@ -174,17 +160,31 @@
 
     lax.fori_loop(0, BLOCKS // 8, chunk_step, 0)
 
-    def order_step(o, carry):
-        index = jnp.broadcast_to(ids_ref[pl.ds(o, 1), :], (8, LANES))
-        acc = gather_blocks(tbl, index >> 7, index & 127)
-        owner, half = slot_place(o)
-        for view in range(VIEWS):
-            row = (view * 32 + owner) * MSG + half
-            out_ref[pl.ds(row, 8, stride=2), :] = acc[view]
-            out_ref[pl.ds(row + 16, 1), :] = acc[4][view : view + 1, :]
+    def turn_step(group, carry):
+        for u in range(4):
+            b = group * 4 + u
+            block = tbl[pl.ds(pl.multiple_of(b * TBL, 8), TBL), :]
+            by_row[pl.ds(pl.multiple_of(b * LANES, 8), LANES), 0:TBL] = block.T
         return carry
 
-    lax.fori_loop(0, BLOCKS, order_step, 0)
+    lax.fori_loop(0, BLOCKS // 4, turn_step, 0)
+    by_row[BLOCKS * LANES : BLOCKS * LANES + 8, :] = jnp.zeros((8, LANES), F32)
+
+    def order_step(group, carry):
+        for u in range(4):
+            o = group * 4 + u
+            for c in range(LANES):
+                stage[u, c : c + 1, :] = by_row[pl.ds(ids_ref[o, c], 1), :]
+        for u in range(4):
+            acc = stage[u, :, 0:TBL].T
+            owner, half = slot_place(group * 4 + u)
+            for view in range(VIEWS):
+                row = (view * 32 + owner) * MSG + half
+                out_ref[pl.ds(row, 8, stride=2), :] = acc[view * 8 : view * 8 + 8, :]
+                out_ref[pl.ds(row + 16, 1), :] = acc[32 + view : 33 + view, :]
+        return carry
+
+    lax.fori_loop(0, BLOCKS // 4, order_step, 0)
 
 
 def top_f32(x):
@@ -206,13 +206,16 @@
 
 
 def tiles(
-    perm_ref, recv_ref, list_ref, target_ref, out_ref, image_ref, loss_ref,
-    tab, wide, target_t, image_t, rec, alpha, weight, ends, shades, prefix, res, behind,
+    perm_ref, recv_ref, list_ref, target_ref, out_ref, image_ref,
+    tab, wide, target_t, image_t, rec, lines, alpha, weight, ends, shades, prefix, res, behind,
     moments, grad, inverse, sums_ref,
 ):
     lane = lax.broadcasted_iota(I32, (8, LANES), 1)
     sub = lax.broadcasted_iota(I32, (8, LANES), 0)
     sub_f = sub.astype(F32)
+    lane_f = lane.astype(F32)
+    rows = lax.broadcasted_iota(I32, (LANES, LANES), 0)
+    wide_lane = lax.broadcasted_iota(I32, (LANES, LANES), 1)
     tall_lane = lax.broadcasted_iota(I32, (256, LANES), 1)
     from_lane = lax.broadcasted_iota(I32, (256, LANES), 0) % 128
     sums_ref[0] = (from_lane < tall_lane).astype(F32).astype(BF16)
@@ -233,7 +236,7 @@
     def take(x, index):
         return jnp.take_along_axis(x, index, axis=1, mode="promise_in_bounds")
 
-    def tile_step(r, loss):
+    def tile_step(r, carry):
         place = perm_ref[r]
         ox = (16 * (place % TW)).astype(F32)
         oy = (16 * (place // TW)).astype(F32)
@@ -244,133 +247,136 @@
             (list_lo >= 0.0).astype(F32) + (list_hi >= 0.0).astype(F32)
         ).astype(I32)
         steps = (count + 127) // 128
+        pairs = (steps + 1) // 2
+        quads = (steps + 3) // 4
         inverse[...] = jnp.zeros_like(inverse)
         tile_rows = pl.multiple_of(r * 16, 8)
 
-        def load_step(j, carry):
-            k = lane * steps + j
-            block, low = k >> 7, k & 127
-            entry = jnp.sum(
-                jnp.where(block == sub, take(list_lo, low), 0.0)
-                + jnp.where(block == sub + 8, take(list_hi, low), 0.0),
-                axis=0,
-                keepdims=True,
-            ).astype(I32)
-            entry = jnp.broadcast_to(entry, (8, LANES))
-            source, slot = (entry >> 8) & 127, entry & 15
-            hit0, hit1 = slot == sub, slot == sub + 8
-            fields = []
+        def load_step(group, carry):
+            many = [group * 4 + u for u in range(4)]
+            entries, masks, records = [], [], []
+            for j in many:
+                k = lane * steps + j
+                block, low = k >> 7, k & 127
+                found = jnp.sum(
+                    jnp.where(block == sub, take(list_lo, low), 0.0)
+                    + jnp.where(block == sub + 8, take(list_hi, low), 0.0),
+                    axis=0,
+                    keepdims=True,
+                ).astype(I32)
+                entries.append(jnp.broadcast_to(jnp.where(j < steps, found, -1), (8, LANES)))
+            for entry in entries:
+                masks.append((entry & 15 == sub, entry & 15 == sub + 8))
+                records.append([])
             for f in range(FIELDS):
-                got0 = take(tab[f, pl.ds(tile_rows, 8), :], source)
-                got1 = take(tab[f, pl.ds(tile_rows + 8, 8), :], source)
-                fields.append(
-                    jnp.sum(
-                        jnp.where(hit0, got0, jnp.where(hit1, got1, 0.0)),
-                        axis=0,
-                        keepdims=True,
+                half0 = tab[f, pl.ds(tile_rows, 8), :]
+                half1 = tab[f, pl.ds(tile_rows + 8, 8), :]
+                for entry, (hit0, hit1), fields in zip(entries, masks, records):
+                    source = (entry >> 8) & 127
+                    got = jnp.where(
+                        hit0, take(half0, source), jnp.where(hit1, take(half1, source), 0.0)
                     )
-                )
-            listed = entry[0:1] >= 0
-            mx, my = fields[0] - ox, fields[1] - oy
-            opacity = jnp.where(listed, fields[5], 1.0)
-            level = jnp.where(listed, jnp.log2(opacity), -1e30)
-            for i, value in enumerate(
-                [mx, my] + fields[2:5] + [opacity] + fields[6:9]
-            ):
-                rec[j, pl.ds(i, 1), :] = value
-            qxx = (-0.5 * LOG2E) * fields[2]
-            qxy = -LOG2E * fields[3]
-            qyy = (-0.5 * LOG2E) * fields[4]
-            parts = []
-            for h in range(2):
-                dx = (sub_f + 8.0 * h) - mx
-                parts.append((qxy * dx, qxx * dx * dx + level))
-            for y in range(16):
-                dy = jnp.broadcast_to(float(y) - my, (8, LANES))
-                turn = qyy * dy
-                for h in range(2):
-                    slope, level_h = parts[h]
-                    alpha[j, y * 2 + h] = jnp.exp2((slope + turn) * dy + level_h)
-            rows = lax.broadcasted_iota(I32, (128, LANES), 0)
-            listed_b = entry >= 0
-            one_hot = (rows == entry[0:1] >> 8).astype(F32)
-            step_no = (j + 1).astype(F32)
-            left = [
-                jnp.where(hit0 & listed_b, step_no, 0.0),
-                jnp.where(hit1 & listed_b, step_no, 0.0),
-                jnp.where(hit0 & listed_b, lane.astype(F32), 0.0),
-                jnp.where(hit1 & listed_b, lane.astype(F32), 0.0),
-            ]
+                    fields.append(jnp.sum(got, axis=0, keepdims=True))
+            lefts, rights = [], []
+            for j, entry, (hit0, hit1) in zip(many, entries, masks):
+                listed = entry >= 0
+                step_no = (j + 1).astype(F32)
+                spots = [jnp.where(listed, step_no, 0.0), jnp.where(listed, lane_f, 0.0)]
+                left = [jnp.where(hit, spot, 0.0) for spot in spots for hit in (hit0, hit1)]
+                lefts.append(jnp.concatenate(left, axis=0).astype(BF16))
+                rights.append((rows == entry[0:1] >> 8).astype(F32).astype(BF16))
             inverse[...] += lax.dot_general(
-                jnp.concatenate(left, axis=0).astype(BF16),
-                one_hot.astype(BF16),
+                jnp.concatenate(lefts, axis=1),
+                jnp.concatenate(rights, axis=1),
                 (((1,), (1,)), ((), ())),
                 preferred_element_type=F32,
             )
+            for j, entry, fields in zip(many, entries, records):
+                listed = entry[0:1] >= 0
+                mx, my = fields[0] - ox, fields[1] - oy
+                opacity = jnp.where(listed, fields[5], 1.0)
+                level = jnp.where(listed, jnp.log2(opacity), -1e30)
+                qyy = (-0.5 * LOG2E) * fields[4]
+                values = [mx, my] + fields[2:5] + [opacity] + fields[6:9] + [qyy]
+                for i, value in enumerate(values):
+                    rec[j, pl.ds(i, 1), :] = value
+                qxx = (-0.5 * LOG2E) * fields[2]
+                qxy = -LOG2E * fields[3]
+                for h in range(2):
+                    dx = (sub_f + 8.0 * h) - mx
+                    lines[j, 2 * h] = qxy * dx
+                    lines[j, 2 * h + 1] = qxx * dx * dx + level
             return carry
 
-        lax.fori_loop(0, steps, load_step, 0)
+        lax.fori_loop(0, quads, load_step, 0)
+
+        def spread(j, i):
+            return jnp.broadcast_to(rec[j, pl.ds(i, 1), :], (8, LANES))
 
         for g in range(4):
 
-            def front_step(j, carry):
+            def front_step(pair, carry):
                 keep, col = list(carry[:8]), list(carry[8:])
-                shade = [
-                    jnp.broadcast_to(rec[j, pl.ds(6 + c, 1), :], (8, LANES)) for c in range(3)
-                ]
-                for i in range(8):
-                    w = alpha[j, g * 8 + i] * keep[i]
-                    weight[j, g * 8 + i] = w
-                    keep[i] = keep[i] - w
-                    for c in range(3):
-                        col[i * 3 + c] = col[i * 3 + c] + shade[c] * w
+                for j in (pair * 2, pair * 2 + 1):
+                    shade = [spread(j, 6 + c) for c in range(3)]
+                    my, qyy = spread(j, 1), spread(j, 9)
+                    slope = [lines[j, 0], lines[j, 2]]
+                    level = [lines[j, 1], lines[j, 3]]
+                    for i in range(8):
+                        if i % 2 == 0:
+                            dy = float(g * 4 + i // 2) - my
+                            turn = qyy * dy
+                        a = jnp.exp2((slope[i % 2] + turn) * dy + level[i % 2])
+                        alpha[j, g * 8 + i] = a
+                        w = a * keep[i]
+                        weight[j, g * 8 + i] = w
+                        keep[i] = keep[i] - w
+                        for c in range(3):
+                            col[i * 3 + c] = col[i * 3 + c] + shade[c] * w
                 return tuple(keep + col)
 
             start = [jnp.ones((8, LANES), F32)] * 8 + [jnp.zeros((8, LANES), F32)] * 24
-            done = lax.fori_loop(0, steps, front_step, tuple(start))
+            done = lax.fori_loop(0, pairs, front_step, tuple(start))
             for i in range(8):
                 ends[g * 8 + i] = done[i]
                 for c in range(3):
                     shades[c, g * 8 + i] = done[8 + i * 3 + c]
 
-        def all_pixels(x):
-            return x.reshape(256, LANES)
-
-        local_end = all_pixels(ends[...])
-        level_end = jnp.log2(local_end)
-        top, rest_bits = split(level_end)
-        low = (rest_bits - top_f32(rest_bits)).astype(BF16)
-        front = jnp.exp2(
-            product(jnp.concatenate([top, rest_bits.astype(BF16)], axis=1), sums_ref[0])
-            + product(low, sums_ref[0, 0:128, :])
-        )
-        prefix[...] = front.reshape(32, 8, LANES)
-        target = target_t[...]
-        image = image_t[...]
-        behind_all = jnp.zeros((256, LANES), F32)
-        square = jnp.zeros((256, LANES), F32)
-        for c in range(3):
-            part = front * all_pixels(shades[c])
-            mine = tall_lane == c * 16 + r
-            diff = summed(part - jnp.where(mine, target, 0.0), sums_ref[1])
-            res[c] = diff.reshape(32, 8, LANES)
-            image = jnp.where(mine, diff + target, image)
-            behind_all = behind_all + diff * part
-            square = square + diff * diff
-        image_t[...] = image
-        behind[...] = (summed(behind_all, sums_ref[2]) / (front * local_end)).reshape(
-            32, 8, LANES
-        )
-        loss = loss + jnp.sum(square.reshape(32, 8, LANES), axis=0)
+        for half in range(2):
+            part_of = slice(half * 16, half * 16 + 16)
+            pixels = slice(half * 128, half * 128 + 128)
+            local_end = ends[part_of].reshape(128, LANES)
+            top, rest = split(jnp.log2(local_end))
+            low = (rest - top_f32(rest)).astype(BF16)
+            front = jnp.exp2(
+                product(jnp.concatenate([top, rest.astype(BF16)], axis=1), sums_ref[0])
+                + product(low, sums_ref[0, 0:128, :])
+            )
+            prefix[part_of] = front.reshape(16, 8, LANES)
+            image = image_t[pixels, :]
+            behind_all = jnp.zeros((128, LANES), F32)
+            for c in range(3):
+                part = front * shades[c, part_of].reshape(128, LANES)
+                mine = wide_lane == c * 16 + r
+                target = target_t[pixels, :]
+                diff = summed(part - jnp.where(mine, target, 0.0), sums_ref[1])
+                res[c, part_of] = diff.reshape(16, 8, LANES)
+                image = jnp.where(mine, diff + target, image)
+                behind_all = behind_all + diff * part
+            image_t[pixels, :] = image
+            behind[part_of] = (summed(behind_all, sums_ref[2]) / (front * local_end)).reshape(
+                16, 8, LANES
+            )
 
         for g in range(4):
 
-            def back_step(back_j, carry):
+            def back_step(back_pair, carry):
+                pair = pairs - 1 - back_pair
+                return one_back(pair * 2, one_back(pair * 2 + 1, carry))
+
+            def one_back(j, carry):
                 back = list(carry)
-                j = steps - 1 - back_j
-                shade = [
-                    jnp.broadcast_to(rec[j, pl.ds(6 + c, 1), :], (8, LANES)) for c in range(3)
-                ]
+                shade = [spread(j, 6 + c) for c in range(3)]
                 if g == 0:
                     sums = [jnp.zeros((8, LANES), F32)] * 9
                 else:
@@ -393,9 +399,14 @@
                     moments[j, i] = sums[i]
                 return tuple(back)
 
-            lax.fori_loop(0, steps, back_step, tuple(behind[g * 8 + i] for i in range(8)))
-
-        def finish_step(j, carry):
+            lax.fori_loop(0, pairs, back_step, tuple(behind[g * 8 + i] for i in range(8)))
+
+        def finish_step(group, carry):
+            for u in range(4):
+                finish(group * 4 + u)
+            return carry
+
+        def finish(j):
             def total(x):
                 return jnp.sum(x, axis=0, keepdims=True)
 
@@ -425,32 +436,34 @@
             ] + [total(s[6 + c]) for c in range(3)]
             for i in range(FIELDS):
                 grad[j, pl.ds(i, 1), :] = out[i]
-            return carry
-
-        lax.fori_loop(0, steps, finish_step, 0)
+
+        lax.fori_loop(0, quads, finish_step, 0)
 
         step0 = inverse[0:8, :].astype(I32)
         step1 = inverse[8:16, :].astype(I32)
         lane0 = inverse[16:24, :].astype(I32)
         lane1 = inverse[24:32, :].astype(I32)
 
-        def unlist_step(j, carry):
+        def unlist_step(group, carry):
             acc = list(carry)
-            hit0, hit1 = step0 == j + 1, step1 == j + 1
-            for f in range(FIELDS):
-                row = jnp.broadcast_to(grad[j, pl.ds(f, 1), :], (8, LANES))
-                acc[2 * f] = jnp.where(hit0, take(row, lane0), acc[2 * f])
-                acc[2 * f + 1] = jnp.where(hit1, take(row, lane1), acc[2 * f + 1])
+            for j in [group * 4 + u for u in range(4)]:
+                hit0, hit1 = step0 == j + 1, step1 == j + 1
+                for f in range(FIELDS):
+                    row = jnp.broadcast_to(grad[j, pl.ds(f, 1), :], (8, LANES))
+                    acc[2 * f] = jnp.where(hit0, take(row, lane0), acc[2 * f])
+                    acc[2 * f + 1] = jnp.where(hit1, take(row, lane1), acc[2 * f + 1])
             return tuple(acc)
 
-        acc = lax.fori_loop(0, steps, unlist_step, (jnp.zeros((8, LANES), F32),) * 18)
+        acc = lax.fori_loop(0, quads, unlist_step, (jnp.zeros((8, LANES), F32),) * 18)
         for f in range(FIELDS):
             tab[f, pl.ds(tile_rows, 8), :] = acc[2 * f]
             tab[f, pl.ds(tile_rows + 8, 8), :] = acc[2 * f + 1]
-        return loss
-
-    loss = lax.fori_loop(0, 16, tile_step, jnp.zeros((8, LANES), F32))
-    loss_ref[...] = loss
+        return carry
+
+    lax.fori_loop(0, 16, tile_step, 0)
+    errors = image_t[...] - target_t[...]
+    total = jnp.sum(errors * errors, axis=0, keepdims=True)
+    out_ref[pl.ds(LOSS_ROW, 128, stride=MSG), :] = jnp.broadcast_to(total, (128, LANES))
     for half in range(2):
         for k in range(FIELDS):
             out_ref[pl.ds(k * 2 + half, 128, stride=MSG), :] = tab[
@@ -463,49 +476,41 @@
 
 def splat_back(
     width_px, height_px, cam_ref, small_ref, harm_ref, ids_ref, ret_ref,
-    gsmall_ref, gharm_ref, tbl, nat, inverse,
+    gsmall_ref, gharm_ref, loss_ref, nat, by_row, stage,
 ):
-    lane = lax.broadcasted_iota(I32, (1, LANES), 1)
-    rows64 = lax.broadcasted_iota(I32, (BLOCKS, LANES), 0)
-    rows128 = lax.broadcasted_iota(I32, (LANES, LANES), 0)
-    inverse[...] = jnp.zeros_like(inverse)
-
-    def invert_step(o, carry):
-        index = ids_ref[pl.ds(o, 1), :]
-        hit = rows64 == index >> 7
-        one_hot = (rows128 == index & 127).astype(F32).astype(BF16)
-        left = jnp.concatenate(
-            [
-                jnp.where(hit, (o + 1).astype(F32), 0.0),
-                jnp.where(hit, lane.astype(F32), 0.0),
-            ],
-            axis=0,
-        )
-        inverse[...] += lax.dot_general(
-            left.astype(BF16),
-            one_hot,
-            (((1,), (1,)), ((), ())),
-            preferred_element_type=F32,
-        )
-        owner, half = slot_place(o)
-        base = o * TBL
-        for view in range(VIEWS):
-            row = (view * 32 + owner) * MSG + half
-            tbl[pl.ds(base + view * 8, 8), :] = ret_ref[pl.ds(row, 8, stride=2), :]
-            tbl[pl.ds(base + 32 + view, 1), :] = ret_ref[pl.ds(row + 16, 1), :]
+    losses = jnp.sum(ret_ref[pl.ds(LOSS_ROW, 128, stride=MSG), :], axis=0, keepdims=True)
+    loss_ref[0, 0] = 0.5 * jnp.sum(losses)
+
+    def clear_step(b, carry):
+        by_row[pl.ds(pl.multiple_of(b * LANES, 8), LANES), :] = jnp.zeros((LANES, LANES), F32)
         return carry
 
-    lax.fori_loop(0, BLOCKS, invert_step, 0)
-
-    def order_step(n, carry):
-        block = jnp.broadcast_to(inverse[pl.ds(n, 1), :].astype(I32) - 1, (8, LANES))
-        low = jnp.broadcast_to(inverse[pl.ds(BLOCKS + n, 1), :].astype(I32), (8, LANES))
-        acc = gather_blocks(tbl, block, low)
-        for i in range(5):
-            nat[pl.ds(8 * i * BLOCKS + n, 8, stride=BLOCKS), :] = acc[i]
+    lax.fori_loop(0, BLOCKS, clear_step, 0)
+
+    def order_step(group, carry):
+        for u in range(4):
+            owner, half = slot_place(group * 4 + u)
+            rows = [(view * 32 + owner) * MSG + half for view in range(VIEWS)]
+            parts = [ret_ref[pl.ds(row, 8, stride=2), :] for row in rows]
+            parts += [ret_ref[pl.ds(row + 16, 1), :] for row in rows]
+            parts.append(jnp.zeros((4, LANES), F32))
+            stage[u, :, 0:TBL] = jnp.concatenate(parts, axis=0).T
+        for u in range(4):
+            for c in range(LANES):
+                by_row[pl.ds(ids_ref[group * 4 + u, c], 1), :] = stage[u, c : c + 1, :]
         return carry
 
-    lax.fori_loop(0, BLOCKS, order_step, 0)
+    lax.fori_loop(0, BLOCKS // 4, order_step, 0)
+
+    def turn_step(group, carry):
+        for u in range(4):
+            n = group * 4 + u
+            block = by_row[pl.ds(pl.multiple_of(n * LANES, 8), LANES), 0:TBL].T
+            for i in range(5):
+                nat[pl.ds(8 * i * BLOCKS + n, 8, stride=BLOCKS), :] = block[8 * i : 8 * i + 8, :]
+        return carry
+
+    lax.fori_loop(0, BLOCKS // 4, turn_step, 0)
 
     def chunk_step(chunk, carry):
         centers = [small_row(small_ref, i, chunk) for i in range(3)]
@@ -603,28 +608,34 @@
     ).reshape(11, BLOCKS, LANES)
     harm = tile_order(harmonic_coeffs)
     ids = tile_order(send_ids[0])
+    ids = jnp.where(ids >= 0, ids, BLOCKS * LANES)
     sending = pl.pallas_call(
         functools.partial(splat_out, width_px, height_px),
         out_shape=shape(128 * MSG, LANES),
-        in_specs=[SM(), VM(), VM(), VM()],
+        in_specs=[SM(), VM(), VM(), SM()],
         out_specs=VM(),
-        scratch_shapes=[pltpu.VMEM((BLOCKS * TBL, LANES), F32)],
+        scratch_shapes=[
+            pltpu.VMEM((BLOCKS * TBL, LANES), F32),
+            pltpu.VMEM((BLOCKS * LANES + 8, LANES), F32),
+            pltpu.VMEM((4, LANES, LANES), F32),
+        ],
         compiler_params=params(32),
         name="splat_out",
     )(cam, small, harm, ids)
     received = exchange(sending)
     vreg = (8, LANES)
-    returning, image, loss = pl.pallas_call(
+    returning, image = pl.pallas_call(
         tiles,
-        out_shape=(shape(128 * MSG, LANES), shape(48, 256), shape(8, LANES)),
+        out_shape=(shape(128 * MSG, LANES), shape(48, 256)),
         in_specs=[SM(), VM(), VM(), VM()],
-        out_specs=(VM(), VM(), VM()),
+        out_specs=(VM(), VM()),
         scratch_shapes=[
             pltpu.VMEM((FIELDS, 256, LANES), F32),
             pltpu.VMEM((LANES, 256), F32),
             pltpu.VMEM((256, LANES), F32),
             pltpu.VMEM((256, LANES), F32),
             pltpu.VMEM((16, 16, LANES), F32),
+            pltpu.VMEM((16, 4) + vreg, F32),
             pltpu.VMEM((16, 32) + vreg, F32),
             pltpu.VMEM((16, 32) + vreg, F32),
             pltpu.VMEM((32,) + vreg, F32),
@@ -646,16 +657,15 @@
         targets[0].transpose(1, 0, 2).reshape(48, 256),
     )
     returned = exchange(returning)
-    total_loss = lax.psum(0.5 * jnp.sum(loss[:, 0]), ("view", "pix"))
-    gsmall, gharm = pl.pallas_call(
+    gsmall, gharm, total_loss = pl.pallas_call(
         functools.partial(splat_back, width_px, height_px),
-        out_shape=(shape(11, BLOCKS, LANES), shape(48 * BLOCKS, LANES)),
-        in_specs=[SM(), VM(), VM(), VM(), VM()],
-        out_specs=(VM(), VM()),
+        out_shape=(shape(11, BLOCKS, LANES), shape(48 * BLOCKS, LANES), shape(1, 1)),
+        in_specs=[SM(), VM(), VM(), SM(), VM()],
+        out_specs=(VM(), VM(), SM()),
         scratch_shapes=[
             pltpu.VMEM((BLOCKS * TBL, LANES), F32),
-            pltpu.VMEM((BLOCKS * TBL, LANES), F32),
-            pltpu.VMEM((2 * BLOCKS, LANES), F32),
+            pltpu.VMEM((BLOCKS * LANES + 8, LANES), F32),
+            pltpu.VMEM((4, LANES, LANES), F32),
         ],
         compiler_params=params(32),
         name="splat_back",
@@ -664,7 +674,7 @@
     rendered = image.reshape(3, 16, 256).transpose(1, 0, 2)[None]
     return (
         rendered,
-        total_loss,
+        total_loss[0, 0],
         flat[0:3],
         flat[3:6],
         flat[6:10],

time: 293 us -> 185 us (0.63)
  Pallas kernels: 139 us -> 89.3 us
  starting transfers between devices: 30.5 us -> 0 us
  blocking collectives: 108 us -> 82.5 us
    psum x1 -> x0, blocking collectives: 74.3 us -> none  [local(): total_loss = lax.psum(0.5 * jnp.sum(loss[:, 0]), ('view', 'pix'))]
    all_to_all x1 -> x2, blocking collectives: 33.4 us -> 82.5 us  [exchange(): lax.all_to_all(blocks, ('view', 'pix'), split_axis=0, concat_axis=0, tile...]
    all_to_all x1 -> x0, starting transfers between devices: 30.5 us -> none  [exchange(): lax.all_to_all(blocks, ('view', 'pix'), split_axis=0, concat_axis=0, tile...]
    pallas_call x1, Pallas kernels: 45.4 us -> 20.5 us  [local(): pl.pallas_call(functools.partial(splat_back, width_px, height_px), out_sh...]
    pallas_call x1, Pallas kernels: 28.6 us -> 13.8 us  [local(): pl.pallas_call(functools.partial(splat_out, width_px, height_px), out_sha...]
    pallas_call x1, Pallas kernels: 65.1 us -> 55 us  [local(): pl.pallas_call(tiles, out_shape=(shape(128 * MSG, LANES), shape(48, 256))...]
  transfers between devices with their start and end apart: 1 -> 0, of which waited for: 0 -> 0; matrix products, arithmetic and copies ran while one was open for 0% -> 0% of each run, Pallas kernels for 0% -> 0%
where the time goes in v2:
time: 185 us; the launch traced here: 182 us
  Pallas kernels  89.3 us (48%)
  blocking collectives  82.5 us (45%)
  local copies, waits for them, and re-layouts  5.75 us (3%)
  other arithmetic  3.3 us (2%)
    all_to_all x2, blocking collectives, exchange(): lax.all_to_all(blocks, ('view', 'pix'), split_axis=0, concat_axis=0, tile...  82.5 us
    pallas_call x1, Pallas kernels, local(): pl.pallas_call(tiles, out_shape=(shape(128 * MSG, LANES), shape(48, 256))...  55 us
    pallas_call x1, Pallas kernels, local(): pl.pallas_call(functools.partial(splat_back, width_px, height_px), out_sh...  20.5 us
    pallas_call x1, Pallas kernels, local(): pl.pallas_call(functools.partial(splat_out, width_px, height_px), out_sha...  13.8 us

profile of v2, /device:TPU:25, one launch (start us, length us, event | category | flops | bytes accessed | tf_op | source)
XLA Modules:
  0.0 181.6 jit_solution(9192357365735290071)
XLA Ops:
  0.6 0.0 copy-start
  0.6 0.9 fusion
  1.5 0.9 add_negate_fusion.1
  2.4 0.9 add_negate_fusion
  3.3 0.8 compare_select_fusion.ids_ref
  4.0 0.9 copy.32
  5.0 1.0 copy_bitcast_fusion.4
  5.9 0.8 pad_maximum_fusion.small_ref
  6.7 0.1 stack.2.cam_ref
  6.8 0.0 copy-done
  6.8 13.8 %splat_out.1 = f32[3072,128]{1,0:T(8,128)S(1)} custom-call(f32[4,16]{1,0:T(4,128)S(1)} %stack.2.cam_ref, f32[11,64,128]{2,1,0:T(8,128)S(1)} %pad_maximum_fusion.small_ref, f32[3072,128]{1,0:T(8,128)S(1)} %bitcast.63, s32[64,128]{1,0:T(8,128)S(1)} %compare_select_fusion.ids_ref), custom_call_target="tpu_custom_call" | custom-call | tf_op jit(solution)/shard_map/splat_out/pallas_call | solution.py:612
  20.7 0.0 copy-start.1
  20.7 0.0 copy-start.2
  20.7 0.0 copy-start.3
  20.7 33.4 %all_to_all.10 = f32[128,24,128]{2,1,0:T(8,128)S(1)} all-to-all(f32[128,24,128]{2,1,0:T(8,128)S(1)} %bitcast.67), channel_id=1, replica_groups=mesh['view'=4,'pix'=32] {'view','pix'}, dimensions={0} | all-to-all | bytes 3145728 | tf_op jit(solution)/shard_map/all_to_all | solution.py:594
  54.1 0.0 copy-done.1
  54.2 0.0 copy-done.2
  54.2 0.0 copy-done.3
  54.2 55.0 %tiles.1 = (f32[3072,128]{1,0:T(8,128)S(1)}, f32[48,256]{1,0:T(8,128)}) custom-call(s32[16]{0:T(128)S(1)} %copy-done.3, f32[3072,128]{1,0:T(8,128)S(1)} %bitcast.66, s32[256,128]{1,0:T(8,128)S(1)} %bitcast.69, f32[48,256]{1,0:T(8,128)S(1)} %bitcast.70), custom_call_target="tpu_custom_call" | custom-call | tf_op jit(solution)/shard_map/tiles/pallas_call | solution.py:627
  109.2 49.1 %all_to_all.11 = f32[128,24,128]{2,1,0:T(8,128)S(1)} all-to-all(f32[128,24,128]{2,1,0:T(8,128)S(1)} %bitcast.68), channel_id=1, replica_groups=mesh['view'=4,'pix'=32] {'view','pix'}, dimensions={0} | all-to-all | bytes 3145728 | tf_op jit(solution)/shard_map/all_to_all | solution.py:594
  158.3 20.5 %splat_back.1 = (f32[11,64,128]{2,1,0:T(8,128)S(1)}, f32[3072,128]{1,0:T(8,128)}, f32[1,1]{1,0:T(1,128)}) custom-call(f32[4,16]{1,0:T(4,128)S(1)} %stack.2.cam_ref, f32[11,64,128]{2,1,0:T(8,128)S(1)} %pad_maximum_fusion.small_ref, f32[3072,128]{1,0:T(8,128)S(1)} %bitcast.64, s32[64,128]{1,0:T(8,128)S(1)} %compare_select_fusion.ids_ref, f32[3072,128]{1,0:T(8,128)S(1)} %bitcast.65), custom_call_target="tpu_custom_call" | custom-call | tf_op jit(solution)/shard_map/splat_back/pallas_call | solution.py:660
  178.8 0.6 slice_bitcast_fusion.3
  179.4 0.7 copy.29
  180.2 0.7 copy.30
  180.9 0.7 copy.31
  (2 shorter events, 0.0 us)
Async XLA Ops:
  0.6 6.2 %copy-start = (f32[48,8192]{1,0:T(8,128)S(1)}, f32[48,8192]{1,0:T(8,128)}, u32[]{:S(2)}) copy-start(f32[48,8192]{1,0:T(8,128)} %param.14) | copy-start | bytes 4718596
  20.7 33.5 %copy-start.1 = (s32[16,2048]{1,0:T(8,128)S(1)}, s32[16,2048]{1,0:T(8,128)}, u32[]{:S(2)}) copy-start(s32[16,2048]{1,0:T(8,128)} %param.17) | copy-start | bytes 393220
  20.7 33.5 %copy-start.2 = (f32[1,16,3,256]{3,1,2,0:T(8,128)S(1)}, f32[1,16,3,256]{3,1,2,0:T(8,128)}, u32[]{:S(2)}) copy-start(f32[1,16,3,256]{3,1,2,0:T(8,128)} %param.19) | copy-start | bytes 147460
  20.7 33.4 %copy-start.3 = (s32[16]{0:T(128)S(1)}, s32[16]{0:T(128)}, u32[]{:S(2)}) copy-start(s32[16]{0:T(128)} %perm_ref.1) | copy-start | bytes 196

commit v3 on v2

--- a/solution.py
+++ b/solution.py
@@ -32,8 +32,7 @@
 LANES = 128
 VIEWS = 4
 FIELDS = 9
-MSG = 24
-LOSS_ROW = 18
+MSG = 16
 TBL = 40
 BLOCKS = 64
 F32 = jnp.float32
@@ -41,18 +40,24 @@
 BF16 = jnp.bfloat16
 
 
-def camera_numbers(cameras):
-    cos, sin = jnp.cos(cameras[:, :3]), jnp.sin(cameras[:, :3])
-    ca, cb, cc = cos[:, 0], cos[:, 1], cos[:, 2]
-    sa, sb, sc = sin[:, 0], sin[:, 1], sin[:, 2]
+def camera_numbers(cameras_ref, cos_ref, sin_ref, cams_ref):
+    for view in range(VIEWS):
+        numbers = one_camera(cameras_ref, cos_ref, sin_ref, view)
+        for i, number in enumerate(numbers):
+            cams_ref[view, i] = number
+
+
+def one_camera(cameras_ref, cos_ref, sin_ref, view):
+    ca, cb, cc = [cos_ref[view, i] for i in range(3)]
+    sa, sb, sc = [sin_ref[view, i] for i in range(3)]
     turn = [
         [cc * cb, cc * sb * sa - sc * ca, cc * sb * ca + sc * sa],
         [sc * cb, sc * sb * sa + cc * ca, sc * sb * ca - cc * sa],
         [-sb, cb * sa, cb * ca],
     ]
-    shift = [cameras[:, 3], cameras[:, 4], cameras[:, 5]]
+    shift = [cameras_ref[view, 3 + i] for i in range(3)]
     anchor = [-sum(turn[i][e] * shift[i] for i in range(3)) for e in range(3)]
-    return jnp.stack(turn[0] + turn[1] + turn[2] + shift + anchor + [shift[0]], axis=1)
+    return turn[0] + turn[1] + turn[2] + shift + anchor
 
 
 def harmonics(x, y, z):
@@ -123,8 +128,14 @@
     return harmonics(*[v * inv for v in off])
 
 
-def small_row(small_ref, index, chunk):
-    return small_ref[index, pl.ds(pl.multiple_of(chunk * 8, 8), 8), :]
+def blocks_of(chunk):
+    return pl.ds(pl.multiple_of(chunk * 8, 8), 8)
+
+
+def load_small(small_ref, chunk):
+    some = blocks_of(chunk)
+    values = [small_ref[i, some, :] for i in range(11)]
+    return values[0:3], values[3:6], values[6:10], jax.nn.sigmoid(values[10])
 
 
 def harm_slice(row, chunk):
@@ -135,16 +146,19 @@
     return (o // 16) * 8 + o % 8, (o // 8) % 2
 
 
-def splat_out(width_px, height_px, cam_ref, small_ref, harm_ref, ids_ref, out_ref, tbl, by_row, stage):
+def splat_out(
+    width_px, height_px, cameras_ref, cos_ref, sin_ref,
+    small_ref, harm_ref, ids_ref,
+    out_ref, last_ref, cams_ref, tbl, by_row, stage,
+):
+    camera_numbers(cameras_ref, cos_ref, sin_ref, cams_ref)
+
     def chunk_step(chunk, carry):
-        centers = [small_row(small_ref, i, chunk) for i in range(3)]
-        scales = [small_row(small_ref, 3 + i, chunk) for i in range(3)]
-        rots = [small_row(small_ref, 6 + i, chunk) for i in range(4)]
-        opacity = jax.nn.sigmoid(small_row(small_ref, 10, chunk))
+        centers, scales, rots, opacity = load_small(small_ref, chunk)
         sigma = shape_of(scales, rots)
         base = chunk * (8 * TBL)
         for view in range(VIEWS):
-            cam = [cam_ref[view, i] for i in range(15)]
+            cam = [cams_ref[view, i] for i in range(15)]
             record = geometry(centers, sigma, cam, width_px, height_px) + [opacity]
             basis = direction_basis(centers, cam)
             for colour in range(3):
@@ -164,11 +178,11 @@
         for u in range(4):
             b = group * 4 + u
             block = tbl[pl.ds(pl.multiple_of(b * TBL, 8), TBL), :]
-            by_row[pl.ds(pl.multiple_of(b * LANES, 8), LANES), 0:TBL] = block.T
+            by_row[pl.ds(pl.multiple_of(b * LANES + 8, 8), LANES), 0:TBL] = block.T
         return carry
 
     lax.fori_loop(0, BLOCKS // 4, turn_step, 0)
-    by_row[BLOCKS * LANES : BLOCKS * LANES + 8, :] = jnp.zeros((8, LANES), F32)
+    by_row[0:8, :] = jnp.zeros((8, LANES), F32)
 
     def order_step(group, carry):
         for u in range(4):
@@ -179,9 +193,9 @@
             acc = stage[u, :, 0:TBL].T
             owner, half = slot_place(group * 4 + u)
             for view in range(VIEWS):
-                row = (view * 32 + owner) * MSG + half
-                out_ref[pl.ds(row, 8, stride=2), :] = acc[view * 8 : view * 8 + 8, :]
-                out_ref[pl.ds(row + 16, 1), :] = acc[32 + view : 33 + view, :]
+                peer = view * 32 + owner
+                out_ref[pl.ds(peer * MSG + half, 8, stride=2), :] = acc[view * 8 : view * 8 + 8, :]
+                last_ref[pl.ds(peer * 2 + half, 1), :] = acc[32 + view : 33 + view, :]
         return carry
 
     lax.fori_loop(0, BLOCKS // 4, order_step, 0)
@@ -206,7 +220,8 @@
 
 
 def tiles(
-    perm_ref, recv_ref, list_ref, target_ref, out_ref, image_ref,
+    perm_ref, recv_ref, recv_last_ref, list_ref, target_ref,
+    out_ref, last_ref, loss_ref, image_ref,
     tab, wide, target_t, image_t, rec, lines, alpha, weight, ends, shades, prefix, res, behind,
     moments, grad, inverse, sums_ref,
 ):
@@ -223,10 +238,13 @@
     sums_ref[2] = (from_lane > tall_lane).astype(F32).astype(BF16)
 
     for half in range(2):
-        for k in range(FIELDS):
+        for k in range(FIELDS - 1):
             tab[k, half * 128 : half * 128 + 128, :] = recv_ref[
                 pl.ds(k * 2 + half, 128, stride=MSG), :
             ].T
+        tab[FIELDS - 1, half * 128 : half * 128 + 128, :] = recv_last_ref[
+            pl.ds(half, 128, stride=2), :
+        ].T
     wide[...] = jnp.zeros_like(wide)
     wide[0:48, :] = target_ref[...]
     for i in range(2):
@@ -463,26 +481,33 @@
     lax.fori_loop(0, 16, tile_step, 0)
     errors = image_t[...] - target_t[...]
     total = jnp.sum(errors * errors, axis=0, keepdims=True)
-    out_ref[pl.ds(LOSS_ROW, 128, stride=MSG), :] = jnp.broadcast_to(total, (128, LANES))
+    loss_ref[...] = jnp.broadcast_to(total, (128, LANES))
     for half in range(2):
-        for k in range(FIELDS):
+        for k in range(FIELDS - 1):
             out_ref[pl.ds(k * 2 + half, 128, stride=MSG), :] = tab[
                 k, half * 128 : half * 128 + 128, :
             ].T
+        last_ref[pl.ds(half, 128, stride=2), :] = tab[
+            FIELDS - 1, half * 128 : half * 128 + 128, :
+        ].T
     for i in range(2):
         wide[:, i * 128 : i * 128 + 128] = image_t[i * 128 : i * 128 + 128, :].T
     image_ref[...] = wide[0:48, :]
 
 
 def splat_back(
-    width_px, height_px, cam_ref, small_ref, harm_ref, ids_ref, ret_ref,
-    gsmall_ref, gharm_ref, loss_ref, nat, by_row, stage,
+    width_px, height_px, cameras_ref, cos_ref, sin_ref,
+    small_ref, harm_ref, ids_ref,
+    ret_ref, ret_last_ref, losses_ref,
+    gsmall_ref, gharm_ref, loss_ref,
+    cams_ref, nat, by_row, stage,
 ):
-    losses = jnp.sum(ret_ref[pl.ds(LOSS_ROW, 128, stride=MSG), :], axis=0, keepdims=True)
+    camera_numbers(cameras_ref, cos_ref, sin_ref, cams_ref)
+    losses = jnp.sum(losses_ref[...], axis=0, keepdims=True)
     loss_ref[0, 0] = 0.5 * jnp.sum(losses)
 
     def clear_step(b, carry):
-        by_row[pl.ds(pl.multiple_of(b * LANES, 8), LANES), :] = jnp.zeros((LANES, LANES), F32)
+        by_row[pl.ds(pl.multiple_of(b * LANES + 8, 8), LANES), :] = jnp.zeros((LANES, LANES), F32)
         return carry
 
     lax.fori_loop(0, BLOCKS, clear_step, 0)
@@ -490,9 +515,9 @@
     def order_step(group, carry):
         for u in range(4):
             owner, half = slot_place(group * 4 + u)
-            rows = [(view * 32 + owner) * MSG + half for view in range(VIEWS)]
-            parts = [ret_ref[pl.ds(row, 8, stride=2), :] for row in rows]
-            parts += [ret_ref[pl.ds(row + 16, 1), :] for row in rows]
+            peers = [view * 32 + owner for view in range(VIEWS)]
+            parts = [ret_ref[pl.ds(peer * MSG + half, 8, stride=2), :] for peer in peers]
+            parts += [ret_last_ref[pl.ds(peer * 2 + half, 1), :] for peer in peers]
             parts.append(jnp.zeros((4, LANES), F32))
             stage[u, :, 0:TBL] = jnp.concatenate(parts, axis=0).T
         for u in range(4):
@@ -505,7 +530,7 @@
     def turn_step(group, carry):
         for u in range(4):
             n = group * 4 + u
-            block = by_row[pl.ds(pl.multiple_of(n * LANES, 8), LANES), 0:TBL].T
+            block = by_row[pl.ds(pl.multiple_of(n * LANES + 8, 8), LANES), 0:TBL].T
             for i in range(5):
                 nat[pl.ds(8 * i * BLOCKS + n, 8, stride=BLOCKS), :] = block[8 * i : 8 * i + 8, :]
         return carry
@@ -513,10 +538,7 @@
     lax.fori_loop(0, BLOCKS // 4, turn_step, 0)
 
     def chunk_step(chunk, carry):
-        centers = [small_row(small_ref, i, chunk) for i in range(3)]
-        scales = [small_row(small_ref, 3 + i, chunk) for i in range(3)]
-        rots = [small_row(small_ref, 6 + i, chunk) for i in range(4)]
-        opacity = jax.nn.sigmoid(small_row(small_ref, 10, chunk))
+        centers, scales, rots, opacity = load_small(small_ref, chunk)
 
         def given(view, i):
             row = view * 8 + i if i < 8 else 32 + view
@@ -527,7 +549,7 @@
         d_sigma = [jnp.zeros((8, LANES), F32)] * 6
         d_opacity = jnp.zeros((8, LANES), F32)
         for view in range(VIEWS):
-            cam = [cam_ref[view, i] for i in range(15)]
+            cam = [cams_ref[view, i] for i in range(15)]
             _, geo_pull = jax.vjp(
                 lambda c, s: geometry(c, s, cam, width_px, height_px), centers, sigma
             )
@@ -552,14 +574,11 @@
             d_centers = [d_centers[e] + d_c[e] + d_dir[e] for e in range(3)]
             d_sigma = [d_sigma[e] + d_s[e] for e in range(6)]
         d_scales, d_rots = shape_pull(d_sigma)
-        values = (
-            list(d_centers)
-            + list(d_scales)
-            + list(d_rots)
-            + [d_opacity * opacity * (1.0 - opacity)]
-        )
-        for i in range(11):
-            gsmall_ref[i, pl.ds(pl.multiple_of(chunk * 8, 8), 8), :] = values[i]
+        some = blocks_of(chunk)
+        values = list(d_centers) + list(d_scales) + list(d_rots)
+        values.append(d_opacity * opacity * (1.0 - opacity))
+        for i, value in enumerate(values):
+            gsmall_ref[i, some, :] = value
         return carry
 
     lax.fori_loop(0, BLOCKS // 8, chunk_step, 0)
@@ -589,11 +608,60 @@
 SM = functools.partial(pl.BlockSpec, memory_space=pltpu.SMEM)
 
 
-def exchange(message):
-    blocks = message.reshape(128, MSG, LANES)
-    return lax.all_to_all(
-        blocks, ("view", "pix"), split_axis=0, concat_axis=0, tiled=True
-    ).reshape(128 * MSG, LANES)
+def exchange_kernel(count, *refs):
+    sources, places = refs[:count], refs[count : 2 * count]
+    sent, arrived, own = refs[2 * count :]
+    view, pix = lax.axis_index("view"), lax.axis_index("pix")
+    me = view * 32 + pix
+    kept = [
+        pltpu.make_async_copy(sources[i].at[me], places[i].at[me], own.at[i])
+        for i in range(count)
+    ]
+    for copy in kept:
+        copy.start()
+
+    def send(step, carry):
+        peer = lax.rem(me + step, 128)
+        for i in range(count):
+            pltpu.make_async_remote_copy(
+                src_ref=sources[i].at[peer],
+                dst_ref=places[i].at[me],
+                send_sem=sent.at[i],
+                recv_sem=arrived.at[i],
+                device_id=(peer // 32, lax.rem(peer, 32)),
+                device_id_type=pl.DeviceIdType.MESH,
+            ).start()
+        return carry
+
+    lax.fori_loop(1, 128, send, 0)
+    for copy in kept:
+        copy.wait()
+    for i in range(count):
+        pltpu.make_async_remote_copy(
+            src_ref=sources[i].at[pl.ds(0, 127)],
+            dst_ref=places[i].at[pl.ds(0, 127)],
+            send_sem=sent.at[i],
+            recv_sem=arrived.at[i],
+            device_id=(view, lax.rem(pix + 1, 32)),
+            device_id_type=pl.DeviceIdType.MESH,
+        ).wait()
+
+
+def exchange(*messages):
+    count = len(messages)
+    blocks = [m.reshape(128, m.shape[0] // 128, LANES) for m in messages]
+    outs = pl.pallas_call(
+        functools.partial(exchange_kernel, count),
+        out_shape=tuple(shape(*b.shape) for b in blocks),
+        in_specs=[VM()] * count,
+        out_specs=(VM(),) * count,
+        scratch_shapes=[pltpu.SemaphoreType.DMA((count,))] * 3,
+        compiler_params=pltpu.CompilerParams(
+            has_side_effects=True, vmem_limit_bytes=16 * 1024 * 1024
+        ),
+        name="exchange",
+    )(*blocks)
+    return [out.reshape(m.shape) for out, m in zip(outs, messages)]
 
 
 def local(
@@ -602,33 +670,34 @@
 ):
     width_px = 16 * TW
     height_px = 16 * (512 // TW)
-    cam = camera_numbers(cameras)
-    small = jnp.concatenate(
-        [centers, log_scales, rotations, logits[None]], axis=0
-    ).reshape(11, BLOCKS, LANES)
+    views = (cameras, jnp.cos(cameras[:, :3]), jnp.sin(cameras[:, :3]))
+    small = jnp.concatenate([centers, log_scales, rotations, logits[None]], axis=0)
+    small = small.reshape(11, BLOCKS, LANES)
     harm = tile_order(harmonic_coeffs)
-    ids = tile_order(send_ids[0])
-    ids = jnp.where(ids >= 0, ids, BLOCKS * LANES)
-    sending = pl.pallas_call(
+    ids = tile_order(send_ids[0]) + 8
+    sending, sending_last = pl.pallas_call(
         functools.partial(splat_out, width_px, height_px),
-        out_shape=shape(128 * MSG, LANES),
-        in_specs=[SM(), VM(), VM(), SM()],
-        out_specs=VM(),
+        out_shape=(shape(128 * MSG, LANES), shape(256, LANES)),
+        in_specs=[SM()] * 3 + [VM()] * 2 + [SM()],
+        out_specs=(VM(), VM()),
         scratch_shapes=[
+            pltpu.SMEM((VIEWS, 16), F32),
             pltpu.VMEM((BLOCKS * TBL, LANES), F32),
             pltpu.VMEM((BLOCKS * LANES + 8, LANES), F32),
             pltpu.VMEM((4, LANES, LANES), F32),
         ],
         compiler_params=params(32),
         name="splat_out",
-    )(cam, small, harm, ids)
-    received = exchange(sending)
+    )(*views, small, harm, ids)
+    received = exchange(sending, sending_last)
     vreg = (8, LANES)
-    returning, image = pl.pallas_call(
+    *returning, image = pl.pallas_call(
         tiles,
-        out_shape=(shape(128 * MSG, LANES), shape(48, 256)),
-        in_specs=[SM(), VM(), VM(), VM()],
-        out_specs=(VM(), VM()),
+        out_shape=(
+            shape(128 * MSG, LANES), shape(256, LANES), shape(128, LANES), shape(48, 256),
+        ),
+        in_specs=[SM(), VM(), VM(), VM(), VM()],
+        out_specs=(VM(), VM(), VM(), VM()),
         scratch_shapes=[
             pltpu.VMEM((FIELDS, 256, LANES), F32),
             pltpu.VMEM((LANES, 256), F32),
@@ -652,24 +721,25 @@
         name="tiles",
     )(
         tile_perm,
-        received,
+        *received,
         tile_order(tile_lists),
         targets[0].transpose(1, 0, 2).reshape(48, 256),
     )
-    returned = exchange(returning)
+    returned = exchange(*returning)
     gsmall, gharm, total_loss = pl.pallas_call(
         functools.partial(splat_back, width_px, height_px),
         out_shape=(shape(11, BLOCKS, LANES), shape(48 * BLOCKS, LANES), shape(1, 1)),
-        in_specs=[SM(), VM(), VM(), SM(), VM()],
+        in_specs=[SM()] * 3 + [VM()] * 2 + [SM()] + [VM()] * 3,
         out_specs=(VM(), VM(), SM()),
         scratch_shapes=[
+            pltpu.SMEM((VIEWS, 16), F32),
             pltpu.VMEM((BLOCKS * TBL, LANES), F32),
             pltpu.VMEM((BLOCKS * LANES + 8, LANES), F32),
             pltpu.VMEM((4, LANES, LANES), F32),
         ],
         compiler_params=params(32),
         name="splat_back",
-    )(cam, small, harm, ids, returned)
+    )(*views, small, harm, ids, *returned)
     flat = gsmall.reshape(11, BLOCKS * LANES)
     rendered = image.reshape(3, 16, 256).transpose(1, 0, 2)[None]
     return (

time: 185 us -> 179 us (0.968); the launches traced: 182 us -> 179 us
  blocking collectives: 82.5 us -> 0 us
  Pallas kernels: 89.3 us -> 169 us
    all_to_all x2 -> x0, blocking collectives: 82.5 us -> none  [exchange(): lax.all_to_all(blocks, ('view', 'pix'), split_axis=0, concat_axis=0, tile...]
    pallas_call x1 -> x3, Pallas kernels: 55 us -> 134 us  [the longest x2 69.3 us: exchange(): pl.pallas_call(functools.partial(exchange_kernel, count), out_shape=tuple...]
    unnamed x14 -> x20, local copies, waits for them, and re-layouts: 3.15 us -> 5.23 us
where the time goes in v3:
time: 179 us
  Pallas kernels  169 us (94%)
  local copies, waits for them, and re-layouts  7.56 us (4%)
    pallas_call x2, Pallas kernels, exchange(): pl.pallas_call(functools.partial(exchange_kernel, count), out_shape=tuple...  69.3 us
    pallas_call x1, Pallas kernels, local(): pl.pallas_call(tiles, out_shape=(shape(128 * MSG, LANES), shape(256, LANE...  65.2 us
    pallas_call x1, Pallas kernels, local(): pl.pallas_call(functools.partial(splat_back, width_px, height_px), out_sh...  20.5 us
    pallas_call x1, Pallas kernels, local(): pl.pallas_call(functools.partial(splat_out, width_px, height_px), out_sha...  14 us
    unnamed x20, local copies, waits for them, and re-layouts  5.23 us

profile of v3, /device:TPU:25, one launch (start us, length us, event | category | flops | bytes accessed | tf_op | source)
XLA Modules:
  0.0 178.8 jit_solution(6857477874759947151)
XLA Ops:
  0.6 0.7 slice_sine_fusion
  1.4 0.8 broadcast_add_fusion
  2.1 0.9 copy.32
  3.0 1.0 copy_bitcast_fusion.4
  4.0 0.8 pad_maximum_fusion.small_ref
  4.8 0.0 copy-start
  4.8 1.4 copy-done
  6.2 0.0 copy-start.4
  6.2 0.7 copy-done.4
  6.9 0.0 copy-start.2
  6.9 0.0 copy-start.3
  6.9 0.0 copy-start.6
  6.9 14.0 %splat_out.1 = (f32[2048,128]{1,0:T(8,128)S(1)}, f32[256,128]{1,0:T(8,128)S(1)}) custom-call(f32[4,6]{1,0:T(4,128)S(1)} %copy-done.4, f32[4,3]{1,0:T(4,128)S(1)} %get-tuple-element.38.cos_ref, f32[4,3]{1,0:T(4,128)S(1)} %get-tuple-element.37.sin_ref, f32[11,64,128]{2,1,0:T(8,128)S(1)} %pad_maximum_fusion.small_ref, f32[3072,128]{1,0:T(8,128)S(1)} %bitcast.69, ...), custom_call_target="tpu_custom_call" | custom-call | tf_op jit(solution)/shard_map/splat_out/pallas_call | solution.py:678
  20.9 33.5 %exchange.2 = (f32[128,16,128]{2,1,0:T(8,128)S(1)}, f32[128,2,128]{2,1,0:T(2,128)S(1)}) custom-call(f32[128,16,128]{2,1,0:T(8,128)S(1)} %bitcast.73, f32[128,2,128]{2,1,0:T(2,128)S(1)} %bitcast.81), custom_call_target="tpu_custom_call" | custom-call | tf_op jit(solution)/shard_map/exchange/pallas_call | solution.py:653
  54.4 0.0 copy-start.1
  54.4 0.0 copy-start.5
  54.4 0.0 copy-done.2
  54.5 0.0 copy-done.3
  54.5 0.0 copy-done.6
  54.5 65.2 %tiles.1 = (f32[2048,128]{1,0:T(8,128)S(1)}, f32[256,128]{1,0:T(8,128)S(1)}, f32[128,128]{1,0:T(8,128)S(1)}, f32[48,256]{1,0:T(8,128)}) custom-call(s32[16]{0:T(128)S(1)} %copy-done.6, f32[2048,128]{1,0:T(8,128)S(1)} %bitcast.72, f32[256,128]{1,0:T(8,128)S(1)} %bitcast.80, s32[256,128]{1,0:T(8,128)S(1)} %bitcast.77, f32[48,256]{1,0:T(8,128)S(1)} %bitcast.84), custom_call_target="tpu_custom_call" | custom-call | tf_op jit(solution)/shard_map/tiles/pallas_call | solution.py:694
  119.6 35.8 %exchange.3 = (f32[128,16,128]{2,1,0:T(8,128)S(1)}, f32[128,2,128]{2,1,0:T(2,128)S(1)}, f32[128,1,128]{2,1,0:T(1,128)S(1)}) custom-call(f32[128,16,128]{2,1,0:T(8,128)S(1)} %bitcast.71, f32[128,2,128]{2,1,0:T(2,128)S(1)} %bitcast.79, f32[128,1,128]{2,1,0:T(1,128)S(1)} %bitcast.83), custom_call_target="tpu_custom_call" | custom-call | tf_op jit(solution)/shard_map/exchange/pallas_call | solution.py:653
  155.4 0.0 copy-done.1
  155.4 0.0 copy-done.5
  155.4 20.5 %splat_back.1 = (f32[11,64,128]{2,1,0:T(8,128)S(1)}, f32[3072,128]{1,0:T(8,128)}, f32[1,1]{1,0:T(1,128)}) custom-call(f32[4,6]{1,0:T(4,128)S(1)} %copy-done.5, f32[4,3]{1,0:T(4,128)S(1)} %get-tuple-element.38.cos_ref, f32[4,3]{1,0:T(4,128)S(1)} %get-tuple-element.37.sin_ref, f32[11,64,128]{2,1,0:T(8,128)S(1)} %pad_maximum_fusion.small_ref, ...), custom_call_target="tpu_custom_call" | custom-call | tf_op jit(solution)/shard_map/splat_back/pallas_call | solution.py:729
  175.9 0.6 slice_bitcast_fusion.3
  176.6 0.7 copy.29
  177.3 0.7 copy.30
  178.1 0.7 copy.31
  (2 shorter events, 0.0 us)
Async XLA Ops:
  4.8 1.4 copy-start
  6.2 0.7 copy-start.4
  6.9 47.5 %copy-start.2 = (s32[16,2048]{1,0:T(8,128)S(1)}, s32[16,2048]{1,0:T(8,128)}, u32[]{:S(2)}) copy-start(s32[16,2048]{1,0:T(8,128)} %param.17) | copy-start | bytes 393220
  6.9 47.5 %copy-start.3 = (f32[1,16,3,256]{3,1,2,0:T(8,128)S(1)}, f32[1,16,3,256]{3,1,2,0:T(8,128)}, u32[]{:S(2)}) copy-start(f32[1,16,3,256]{3,1,2,0:T(8,128)} %param.19) | copy-start | bytes 147460
  6.9 47.6 %copy-start.6 = (s32[16]{0:T(128)S(1)}, s32[16]{0:T(128)}, u32[]{:S(2)}) copy-start(s32[16]{0:T(128)} %perm_ref.1) | copy-start | bytes 196
  54.4 101.0 %copy-start.1 = (f32[48,8192]{1,0:T(8,128)S(1)}, f32[48,8192]{1,0:T(8,128)}, u32[]{:S(2)}) copy-start(f32[48,8192]{1,0:T(8,128)} %param.14) | copy-start | bytes 4718596
  54.4 101.0 %copy-start.5 = (f32[4,6]{1,0:T(4,128)S(1)}, f32[4,6]{1,0:T(4,128)}, u32[]{:S(2)}) copy-start(f32[4,6]{1,0:T(4,128)} %cameras_ref.3) | copy-start | bytes 292

commit v4 on v3

--- a/solution.py
+++ b/solution.py
@@ -128,12 +128,8 @@
     return harmonics(*[v * inv for v in off])
 
 
-def blocks_of(chunk):
-    return pl.ds(pl.multiple_of(chunk * 8, 8), 8)
-
-
 def load_small(small_ref, chunk):
-    some = blocks_of(chunk)
+    some = pl.ds(pl.multiple_of(chunk * 8, 8), 8)
     values = [small_ref[i, some, :] for i in range(11)]
     return values[0:3], values[3:6], values[6:10], jax.nn.sigmoid(values[10])
 
@@ -144,12 +140,26 @@
 
 def slot_place(o):
     return (o // 16) * 8 + o % 8, (o // 8) % 2
+
+
+def alternate(fill, drain, stage_a, stage_b):
+    groups = BLOCKS // 2
+    fill(stage_a, 0)
+
+    def step(pair, carry):
+        fill(stage_b, pair * 2 + 1)
+        drain(stage_a, pair * 2)
+        fill(stage_a, jnp.minimum(pair * 2 + 2, groups - 1))
+        drain(stage_b, pair * 2 + 1)
+        return carry
+
+    lax.fori_loop(0, groups // 2, step, 0)
 
 
 def splat_out(
     width_px, height_px, cameras_ref, cos_ref, sin_ref,
     small_ref, harm_ref, ids_ref,
-    out_ref, last_ref, cams_ref, tbl, by_row, stage,
+    out_ref, last_ref, cams_ref, tbl, by_row, stage_a, stage_b,
 ):
     camera_numbers(cameras_ref, cos_ref, sin_ref, cams_ref)
 
@@ -184,21 +194,21 @@
     lax.fori_loop(0, BLOCKS // 4, turn_step, 0)
     by_row[0:8, :] = jnp.zeros((8, LANES), F32)
 
-    def order_step(group, carry):
-        for u in range(4):
-            o = group * 4 + u
+    def fill(stage, group):
+        for u in range(2):
             for c in range(LANES):
-                stage[u, c : c + 1, :] = by_row[pl.ds(ids_ref[o, c], 1), :]
-        for u in range(4):
+                stage[u, c : c + 1, :] = by_row[pl.ds(ids_ref[group * 2 + u, c] + 8, 1), :]
+
+    def drain(stage, group):
+        for u in range(2):
             acc = stage[u, :, 0:TBL].T
-            owner, half = slot_place(group * 4 + u)
+            owner, half = slot_place(group * 2 + u)
             for view in range(VIEWS):
                 peer = view * 32 + owner
                 out_ref[pl.ds(peer * MSG + half, 8, stride=2), :] = acc[view * 8 : view * 8 + 8, :]
                 last_ref[pl.ds(peer * 2 + half, 1), :] = acc[32 + view : 33 + view, :]
-        return carry
-
-    lax.fori_loop(0, BLOCKS // 4, order_step, 0)
+
+    alternate(fill, drain, stage_a, stage_b)
 
 
 def top_f32(x):
@@ -230,7 +240,6 @@
     sub_f = sub.astype(F32)
     lane_f = lane.astype(F32)
     rows = lax.broadcasted_iota(I32, (LANES, LANES), 0)
-    wide_lane = lax.broadcasted_iota(I32, (LANES, LANES), 1)
     tall_lane = lax.broadcasted_iota(I32, (256, LANES), 1)
     from_lane = lax.broadcasted_iota(I32, (256, LANES), 0) % 128
     sums_ref[0] = (from_lane < tall_lane).astype(F32).astype(BF16)
@@ -360,31 +369,32 @@
                 for c in range(3):
                     shades[c, g * 8 + i] = done[8 + i * 3 + c]
 
-        for half in range(2):
-            part_of = slice(half * 16, half * 16 + 16)
-            pixels = slice(half * 128, half * 128 + 128)
-            local_end = ends[part_of].reshape(128, LANES)
-            top, rest = split(jnp.log2(local_end))
-            low = (rest - top_f32(rest)).astype(BF16)
-            front = jnp.exp2(
-                product(jnp.concatenate([top, rest.astype(BF16)], axis=1), sums_ref[0])
-                + product(low, sums_ref[0, 0:128, :])
-            )
-            prefix[part_of] = front.reshape(16, 8, LANES)
-            image = image_t[pixels, :]
-            behind_all = jnp.zeros((128, LANES), F32)
-            for c in range(3):
-                part = front * shades[c, part_of].reshape(128, LANES)
-                mine = wide_lane == c * 16 + r
-                target = target_t[pixels, :]
-                diff = summed(part - jnp.where(mine, target, 0.0), sums_ref[1])
-                res[c, part_of] = diff.reshape(16, 8, LANES)
-                image = jnp.where(mine, diff + target, image)
-                behind_all = behind_all + diff * part
-            image_t[pixels, :] = image
-            behind[part_of] = (summed(behind_all, sums_ref[2]) / (front * local_end)).reshape(
-                16, 8, LANES
-            )
+        local_end = ends[...].reshape(256, LANES)
+        top, rest = split(jnp.log2(local_end))
+        low = (rest - top_f32(rest)).astype(BF16)
+        front = jnp.exp2(
+            product(jnp.concatenate([top, rest.astype(BF16)], axis=1), sums_ref[0])
+            + product(low, sums_ref[0, 0:128, :])
+        )
+        prefix[...] = front.reshape(32, 8, LANES)
+        parts = [front * shades[c].reshape(256, LANES) for c in range(3)]
+        target = target_t[...]
+        masks = [tall_lane == c * 16 + r for c in range(3)]
+        diffs = [
+            jnp.sum(part - jnp.where(mine, target, 0.0), axis=1, keepdims=True)
+            for part, mine in zip(parts, masks)
+        ]
+        image = image_t[...]
+        behind_all = jnp.zeros((256, LANES), F32)
+        for c in range(3):
+            diff = jnp.broadcast_to(diffs[c], (256, LANES))
+            res[c] = diff.reshape(32, 8, LANES)
+            image = jnp.where(masks[c], diff + target, image)
+            behind_all = behind_all + diff * parts[c]
+        image_t[...] = image
+        behind[...] = (summed(behind_all, sums_ref[2]) / (front * local_end)).reshape(
+            32, 8, LANES
+        )
 
         for g in range(4):
 
@@ -464,12 +474,14 @@
 
         def unlist_step(group, carry):
             acc = list(carry)
-            for j in [group * 4 + u for u in range(4)]:
-                hit0, hit1 = step0 == j + 1, step1 == j + 1
+            many = [group * 4 + u for u in range(4)]
+            for half, (step_of, lane_of) in enumerate(((step0, lane0), (step1, lane1))):
                 for f in range(FIELDS):
-                    row = jnp.broadcast_to(grad[j, pl.ds(f, 1), :], (8, LANES))
-                    acc[2 * f] = jnp.where(hit0, take(row, lane0), acc[2 * f])
-                    acc[2 * f + 1] = jnp.where(hit1, take(row, lane1), acc[2 * f + 1])
+                    value = acc[2 * f + half]
+                    for j in many:
+                        row = jnp.broadcast_to(grad[j, pl.ds(f, 1), :], (8, LANES))
+                        value = jnp.where(step_of == j + 1, take(row, lane_of), value)
+                    acc[2 * f + half] = value
             return tuple(acc)
 
         acc = lax.fori_loop(0, quads, unlist_step, (jnp.zeros((8, LANES), F32),) * 18)
@@ -522,7 +534,7 @@
             stage[u, :, 0:TBL] = jnp.concatenate(parts, axis=0).T
         for u in range(4):
             for c in range(LANES):
-                by_row[pl.ds(ids_ref[group * 4 + u, c], 1), :] = stage[u, c : c + 1, :]
+                by_row[pl.ds(ids_ref[group * 4 + u, c] + 8, 1), :] = stage[u, c : c + 1, :]
         return carry
 
     lax.fori_loop(0, BLOCKS // 4, order_step, 0)
@@ -574,11 +586,10 @@
             d_centers = [d_centers[e] + d_c[e] + d_dir[e] for e in range(3)]
             d_sigma = [d_sigma[e] + d_s[e] for e in range(6)]
         d_scales, d_rots = shape_pull(d_sigma)
-        some = blocks_of(chunk)
         values = list(d_centers) + list(d_scales) + list(d_rots)
         values.append(d_opacity * opacity * (1.0 - opacity))
         for i, value in enumerate(values):
-            gsmall_ref[i, some, :] = value
+            gsmall_ref[harm_slice(i, chunk), :] = value
         return carry
 
     lax.fori_loop(0, BLOCKS // 8, chunk_step, 0)
@@ -674,7 +685,7 @@
     small = jnp.concatenate([centers, log_scales, rotations, logits[None]], axis=0)
     small = small.reshape(11, BLOCKS, LANES)
     harm = tile_order(harmonic_coeffs)
-    ids = tile_order(send_ids[0]) + 8
+    ids = tile_order(send_ids[0])
     sending, sending_last = pl.pallas_call(
         functools.partial(splat_out, width_px, height_px),
         out_shape=(shape(128 * MSG, LANES), shape(256, LANES)),
@@ -684,7 +695,8 @@
             pltpu.SMEM((VIEWS, 16), F32),
             pltpu.VMEM((BLOCKS * TBL, LANES), F32),
             pltpu.VMEM((BLOCKS * LANES + 8, LANES), F32),
-            pltpu.VMEM((4, LANES, LANES), F32),
+            pltpu.VMEM((2, LANES, LANES), F32),
+            pltpu.VMEM((2, LANES, LANES), F32),
         ],
         compiler_params=params(32),
         name="splat_out",
@@ -728,7 +740,7 @@
     returned = exchange(*returning)
     gsmall, gharm, total_loss = pl.pallas_call(
         functools.partial(splat_back, width_px, height_px),
-        out_shape=(shape(11, BLOCKS, LANES), shape(48 * BLOCKS, LANES), shape(1, 1)),
+        out_shape=(shape(16 * BLOCKS, LANES), shape(48 * BLOCKS, LANES), shape(1, 1)),
         in_specs=[SM()] * 3 + [VM()] * 2 + [SM()] + [VM()] * 3,
         out_specs=(VM(), VM(), SM()),
         scratch_shapes=[
@@ -740,7 +752,7 @@
         compiler_params=params(32),
         name="splat_back",
     )(*views, small, harm, ids, *returned)
-    flat = gsmall.reshape(11, BLOCKS * LANES)
+    flat = from_tile_order(gsmall, 16)
     rendered = image.reshape(3, 16, 256).transpose(1, 0, 2)[None]
     return (
         rendered,

time: 179 us -> 171 us (0.955)
  Pallas kernels: 169 us -> 161 us
    pallas_call x1, Pallas kernels: 65.2 us -> 59.5 us  [local(): pl.pallas_call(tiles, out_shape=(shape(128 * MSG, LANES), shape(256, LANE...]
    slice x0 -> x3, local copies, waits for them, and re-layouts: none -> 2.07 us  [the longest x1 0.74 us: local(): flat[3:6]]
    unnamed x20 -> x19, local copies, waits for them, and re-layouts: 5.23 us -> 3.79 us
where the time goes in v4:
time: 171 us; the launch traced here: 170 us
  Pallas kernels  161 us (94%)
  local copies, waits for them, and re-layouts  7.56 us (4%)
    pallas_call x2, Pallas kernels, exchange(): pl.pallas_call(functools.partial(exchange_kernel, count), out_shape=tuple...  67.5 us
    pallas_call x1, Pallas kernels, local(): pl.pallas_call(tiles, out_shape=(shape(128 * MSG, LANES), shape(256, LANE...  59.5 us
    pallas_call x1, Pallas kernels, local(): pl.pallas_call(functools.partial(splat_back, width_px, height_px), out_sh...  20.5 us
    pallas_call x1, Pallas kernels, local(): pl.pallas_call(functools.partial(splat_out, width_px, height_px), out_sha...  13.5 us
    unnamed x19, local copies, waits for them, and re-layouts  3.79 us

profile of v4, /device:TPU:25, one launch (start us, length us, event | category | flops | bytes accessed | tf_op | source)
XLA Modules:
  0.0 170.2 jit_solution(9380460990290032195)
XLA Ops:
  0.6 0.7 slice_sine_fusion
  1.4 0.9 copy.23
  2.3 1.0 copy_bitcast_fusion.1
  3.3 0.8 pad_maximum_fusion.small_ref
  4.1 0.0 copy-start
  4.1 1.4 copy-done
  5.5 0.0 copy-start.2
  5.5 0.8 copy-done.2
  6.2 0.0 copy-start.6
  6.2 0.7 copy-done.6
  6.9 0.0 copy-start.4
  6.9 0.0 copy-start.5
  6.9 0.0 copy-start.8
  6.9 13.5 %splat_out.1 = (f32[2048,128]{1,0:T(8,128)S(1)}, f32[256,128]{1,0:T(8,128)S(1)}) custom-call(f32[4,6]{1,0:T(4,128)S(1)} %copy-done.6, f32[4,3]{1,0:T(4,128)S(1)} %get-tuple-element.38.cos_ref, f32[4,3]{1,0:T(4,128)S(1)} %get-tuple-element.37.sin_ref, f32[11,64,128]{2,1,0:T(8,128)S(1)} %pad_maximum_fusion.small_ref, f32[3072,128]{1,0:T(8,128)S(1)} %bitcast.58, ...), custom_call_target="tpu_custom_call" | custom-call | tf_op jit(solution)/shard_map/splat_out/pallas_call | solution.py:689
  20.4 33.5 %exchange.2 = (f32[128,16,128]{2,1,0:T(8,128)S(1)}, f32[128,2,128]{2,1,0:T(2,128)S(1)}) custom-call(f32[128,16,128]{2,1,0:T(8,128)S(1)} %bitcast.62, f32[128,2,128]{2,1,0:T(2,128)S(1)} %bitcast.73), custom_call_target="tpu_custom_call" | custom-call | tf_op jit(solution)/shard_map/exchange/pallas_call | solution.py:664
  53.9 0.0 copy-start.1
  54.0 0.0 copy-start.3
  54.0 0.0 copy-start.7
  54.0 0.0 copy-done.4
  54.0 0.0 copy-done.5
  54.0 0.0 copy-done.8
  54.0 59.5 %tiles.1 = (f32[2048,128]{1,0:T(8,128)S(1)}, f32[256,128]{1,0:T(8,128)S(1)}, f32[128,128]{1,0:T(8,128)S(1)}, f32[48,256]{1,0:T(8,128)}) custom-call(s32[16]{0:T(128)S(1)} %copy-done.8, f32[2048,128]{1,0:T(8,128)S(1)} %bitcast.61, f32[256,128]{1,0:T(8,128)S(1)} %bitcast.72, s32[256,128]{1,0:T(8,128)S(1)} %bitcast.69, f32[48,256]{1,0:T(8,128)S(1)} %bitcast.76), custom_call_target="tpu_custom_call" | custom-call | tf_op jit(solution)/shard_map/tiles/pallas_call | solution.py:706
  113.5 34.1 %exchange.3 = (f32[128,16,128]{2,1,0:T(8,128)S(1)}, f32[128,2,128]{2,1,0:T(2,128)S(1)}, f32[128,1,128]{2,1,0:T(1,128)S(1)}) custom-call(f32[128,16,128]{2,1,0:T(8,128)S(1)} %bitcast.60, f32[128,2,128]{2,1,0:T(2,128)S(1)} %bitcast.71, f32[128,1,128]{2,1,0:T(1,128)S(1)} %bitcast.75), custom_call_target="tpu_custom_call" | custom-call | tf_op jit(solution)/shard_map/exchange/pallas_call | solution.py:664
  147.5 0.0 copy-done.1
  147.6 0.0 copy-done.3
  147.6 0.0 copy-done.7
  147.6 20.5 %splat_back.1 = (f32[1024,128]{1,0:T(8,128)S(1)}, f32[3072,128]{1,0:T(8,128)}, f32[1,1]{1,0:T(1,128)}) custom-call(f32[4,6]{1,0:T(4,128)S(1)} %copy-done.7, f32[4,3]{1,0:T(4,128)S(1)} %get-tuple-element.38.cos_ref, f32[4,3]{1,0:T(4,128)S(1)} %get-tuple-element.37.sin_ref, f32[11,64,128]{2,1,0:T(8,128)S(1)} %pad_maximum_fusion.small_ref, ...), custom_call_target="tpu_custom_call" | custom-call | tf_op jit(solution)/shard_map/splat_back/pallas_call | solution.py:741
  168.1 0.6 slice.24
  168.8 0.7 slice.23
  169.4 0.7 fusion
Async XLA Ops:
  4.1 1.4 copy-start
  5.5 0.8 copy-start.2
  6.2 0.7 copy-start.6
  6.9 47.1 %copy-start.4 = (s32[16,2048]{1,0:T(8,128)S(1)}, s32[16,2048]{1,0:T(8,128)}, u32[]{:S(2)}) copy-start(s32[16,2048]{1,0:T(8,128)} %param.17) | copy-start | bytes 393220
  6.9 47.1 %copy-start.5 = (f32[1,16,3,256]{3,1,2,0:T(8,128)S(1)}, f32[1,16,3,256]{3,1,2,0:T(8,128)}, u32[]{:S(2)}) copy-start(f32[1,16,3,256]{3,1,2,0:T(8,128)} %param.19) | copy-start | bytes 147460
  6.9 47.1 %copy-start.8 = (s32[16]{0:T(128)S(1)}, s32[16]{0:T(128)}, u32[]{:S(2)}) copy-start(s32[16]{0:T(128)} %perm_ref.1) | copy-start | bytes 196
  53.9 93.6 %copy-start.1 = (f32[48,8192]{1,0:T(8,128)S(1)}, f32[48,8192]{1,0:T(8,128)}, u32[]{:S(2)}) copy-start(f32[48,8192]{1,0:T(8,128)} %param.14) | copy-start | bytes 4718596
  54.0 93.6 %copy-start.3 = (s32[1,32,256]{2,1,0:T(8,128)S(1)}, s32[1,32,256]{2,1,0:T(8,128)}, u32[]{:S(2)}) copy-start(s32[1,32,256]{2,1,0:T(8,128)} %param.16) | copy-start | bytes 98308
  54.0 93.6 %copy-start.7 = (f32[4,6]{1,0:T(4,128)S(1)}, f32[4,6]{1,0:T(4,128)}, u32[]{:S(2)}) copy-start(f32[4,6]{1,0:T(4,128)} %cameras_ref.3) | copy-start | bytes 292
